TPU v7x, 512 devices: a whole 4x8x8 slice. The times are simulated.
512 devices in a mesh: seg: 32 (over y, x), head: 16 (over z, core).
Axes of the slice: x: 4, y: 8, z: 8, core: 2. Of those that a mesh axis runs over, the one named last changes fastest.
Arguments:
- queries: bfloat16 [32768, 2048], P(('seg', 'head')), may hold values from -6 to 6
- key_states: bfloat16 [32768, 2048], P(('seg', 'head')), may hold values from -6 to 6
- value_states: bfloat16 [32768, 2048], P(('seg', 'head')), may hold values from -6 to 6
- offsets: int32 [32, 6], P('head'), may hold values from 0 to 31, as said below
Outputs:
- attended: bfloat16 [32768, 2048], P(('seg', 'head'))
Inputs may be any that keep to these rules, and one draw needn't show every extreme that they name: offsets[h, l] lies in 0 .. 2^l - 1, and at each level every value of that range is taken by the same number of heads.
All inputs are finite; a program needn't handle non-finite values.
Results may differ from a plain program's by a relative error of at most 0.0044.
Values may be sent and summed in bfloat16 or wider, within the bound.
A program may use at most 64 MiB of HBM per device.

v0:
```python
import math

import jax
import jax.numpy as jnp
from jax import lax
from jax.sharding import PartitionSpec as P

D = 2048
H = 32


def from_partner(block, axis, apart):
    count = lax.axis_size(axis)
    route = []
    for low in range(count):
        high = low | 1 << apart
        if high != low and high < count:
            route += [(low, high), (high, low)]
    return lax.ppermute(block, axis, route)


def attend_block(query_block, key_block, value_block, score_scale, heads, head_dim):
    query_view = query_block.reshape(query_block.shape[0], heads, head_dim)
    key_view = key_block.reshape(key_block.shape[0], heads, head_dim)
    value_view = value_block.reshape(value_block.shape[0], heads, head_dim)
    scores = (
        jnp.einsum("qhe,khe->hqk", query_view, key_view, preferred_element_type=jnp.float32)
        * score_scale
    )
    row_max = jnp.max(scores, axis=-1)
    expo = jnp.exp(scores - row_max[..., None])
    denom = jnp.sum(expo, axis=-1)
    probs = expo.astype(jnp.bfloat16)
    summed = jnp.einsum("hqk,khe->qhe", probs, value_view, preferred_element_type=jnp.float32)
    level_out = summed / jnp.transpose(denom)[..., None]
    lse = row_max + jnp.log(denom)
    return (level_out.reshape(query_block.shape[0], heads * head_dim), jnp.transpose(lse))


def attend_rows(query_rows, key_rows, value_rows, score_scale, heads, head_dim):
    total = query_rows.shape[0]
    part_count = max(1, total // 512)
    while total % part_count:
        part_count -= 1
    shaped = query_rows.reshape(part_count, total // part_count, query_rows.shape[1])
    level_out, lse = lax.map(
        lambda piece: attend_block(piece, key_rows, value_rows, score_scale, heads, head_dim),
        shaped,
    )
    return (level_out.reshape(total, level_out.shape[-1]), lse.reshape(total, lse.shape[-1]))


def per_device(queries, key_states, value_states, offsets):
    query_all, key_all, value_all = (
        lax.all_to_all(queries, "head", split_axis=1, concat_axis=0, tiled=True),
        lax.all_to_all(key_states, "head", split_axis=1, concat_axis=0, tiled=True),
        lax.all_to_all(value_states, "head", split_axis=1, concat_axis=0, tiled=True),
    )
    row_total = query_all.shape[0]
    width = query_all.shape[1]
    head_dim = D // H
    heads = width // head_dim
    levels = offsets.shape[1]
    score_scale = 1.0 / math.sqrt(head_dim)
    column_head = jnp.arange(width) // head_dim

    def column_mask(level_id):
        return jnp.arange(2**level_id)[:, None] == offsets[:, level_id][column_head][None, :]

    def pick_rows(field, level_id):
        stride = 2**level_id
        shaped = field.reshape(row_total // stride, stride, width)
        mask = column_mask(level_id)
        return jnp.sum(jnp.where(mask[None], shaped, jnp.zeros_like(shaped)), axis=1)

    def packed_rows(level_id):
        return jnp.concatenate(
            [pick_rows(key_all, level_id), pick_rows(value_all, level_id)], axis=1
        )

    def attend_packed(level_id, gathered):
        return attend_rows(
            pick_rows(query_all, level_id),
            gathered[:, :width],
            gathered[:, width:],
            score_scale,
            heads,
            head_dim,
        )

    lower_rows = {}
    for level_id in range(1, levels - 1):
        lower_rows[level_id] = packed_rows(level_id)
    for level_id in range(1, levels - 1):
        current = lower_rows[level_id]
        for bit_index in range(level_id):
            current = jnp.concatenate([current, from_partner(current, "seg", bit_index)], axis=0)
        lower_rows[level_id] = current
    results = [attend_rows(query_all, key_all, value_all, score_scale, heads, head_dim)]
    for level_id in range(1, levels - 1):
        results.append(attend_packed(level_id, lower_rows[level_id]))
    top_level = levels - 1
    top_packed = packed_rows(top_level)
    current = top_packed
    for bit_index in range(top_level):
        current = jnp.concatenate([current, from_partner(current, "seg", bit_index)], axis=0)
    results.append(attend_packed(top_level, current))
    for level_id in range(levels):
        level_out, lse = results[level_id]
        mask = column_mask(level_id)
        lse_columns = jnp.repeat(lse, head_dim, axis=1)
        full_out = (level_out[:, None, :] * mask[None].astype(jnp.float32)).reshape(
            row_total, width
        )
        full_lse = jnp.where(mask[None], lse_columns[:, None, :], jnp.float32(-jnp.inf)).reshape(
            row_total, width
        )
        if level_id == 0:
            best_lse = full_lse
            weight_sum = jnp.ones_like(full_lse)
            accum = full_out
        else:
            new_best = jnp.maximum(best_lse, full_lse)
            fade = jnp.exp(best_lse - new_best)
            weight = jnp.exp(full_lse - new_best)
            accum = accum * fade + weight * full_out
            weight_sum = weight_sum * fade + weight
            best_lse = new_best
    merged = (accum / weight_sum).astype(jnp.bfloat16)
    return lax.all_to_all(merged, "head", split_axis=0, concat_axis=1, tiled=True)


def solution(mesh):
    placed = (
        P(("seg", "head"), None),
        P(("seg", "head"), None),
        P(("seg", "head"), None),
        P("head", None),
    )
    return jax.shard_map(
        per_device, mesh=mesh, in_specs=placed, out_specs=P(("seg", "head"), None), check_vma=False
    )
```

profile of v0, /device:TPU:1, one launch (start us, length us, event | category | flops | bytes accessed | tf_op | source)
XLA Modules:
  0.0 180.5 jit_solution(14794178639039363594)
XLA Ops:
  1.7 11.8 %all-to-all-start = ((bf16[64,16,128]{2,0,1:T(8,128)(2,1)}), bf16[64,16,128]{2,0,1:T(8,128)(2,1)S(1)}, u32[]{:S(2)}, u32[]{:S(2)}) async-start(bf16[64,16,128]{2,0,1:T(8,128)(2,1)} %copy_bitcast_fusion.3), calls=%async_computation | async-start | bytes 524288 | tf_op jit(solution)/shard_map/all_to_all | solution.py:55
  13.6 1.8 %fusion.90 = (s32[1,1]{1,0:T(1,128)}, s32[1,1]{1,0:T(1,128)}, s32[1,1]{1,0:T(1,128)}, s32[1,1]{1,0:T(1,128)}, s32[1,1]{1,0:T(1,128)}, /*index=5*/s32[1,1]{1,0:T(...) fusion(s32[2,6]{1,0:T(2,128)} %param.9), kind=kLoop, calls=%fused_computation.194 | loop fusion | bytes 96 | tf_op jit(solution)/shard_map/gather | solution.py:68
  17.3 1.7 fusion.84
  22.1 1.7 copy_bitcast_fusion.2
  25.3 5.8 %all-to-all-start.1 = ((bf16[64,16,128]{2,0,1:T(8,128)(2,1)}), bf16[64,16,128]{2,0,1:T(8,128)(2,1)S(1)}, u32[]{:S(2)}, u32[]{:S(2)}) async-start(bf16[64,16,128]{2,0,1:T(8,128)(2,1)} %copy_bitcast_fusion.2), calls=%async_computation.1 | async-start | bytes 524288 | tf_op jit(solution)/shard_map/all_to_all | solution.py:56
  32.8 1.7 copy_bitcast_fusion.1
  34.5 8.2 %all-to-all-done.1 = bf16[64,16,128]{2,0,1:T(8,128)(2,1)S(1)} async-done(((bf16[64,16,128]{2,0,1:T(8,128)(2,1)}), bf16[64,16,128]{2,0,1:T(8,128)(2,1)S(1)}, u32[]{:S(2)}, u32[]{:S(2)}) %all-to-all-start.1) | async-done | bytes 262176 | tf_op jit(solution)/shard_map/all_to_all | solution.py:56
  42.8 3.4 %all-to-all-start.2 = ((bf16[64,16,128]{2,0,1:T(8,128)(2,1)}), bf16[64,16,128]{2,0,1:T(8,128)(2,1)S(1)}, u32[]{:S(2)}, u32[]{:S(2)}) async-start(bf16[64,16,128]{2,0,1:T(8,128)(2,1)} %copy_bitcast_fusion.1), calls=%async_computation.2 | async-start | bytes 524288 | tf_op jit(solution)/shard_map/all_to_all | solution.py:57
  48.9 8.4 %all-to-all-done.2 = bf16[64,16,128]{2,0,1:T(8,128)(2,1)S(1)} async-done(((bf16[64,16,128]{2,0,1:T(8,128)(2,1)}), bf16[64,16,128]{2,0,1:T(8,128)(2,1)S(1)}, u32[]{:S(2)}, u32[]{:S(2)}) %all-to-all-start.2) | async-done | bytes 262176 | tf_op jit(solution)/shard_map/all_to_all | solution.py:57
  60.6 3.1 %collective-permute-start.3 = (bf16[128,256]{1,0:T(8,128)(2,1)S(1)}, bf16[128,256]{1,0:T(8,128)(2,1)S(1)}, u32[]{:S(2)}, u32[]{:S(2)}) collective-permute-start(bf16[128,256]{1,0:T(8,128)(2,1)S(1)} %pad_maximum_fusion.11), channel_id=1, source_target_pairs={{0,16},{16,0},{32,48},{48,32},{64,80},{80,64},{96,112},{112,96},{1... | collective-permute-start | bytes 196616 | tf_op jit(solution)/shard_map/ppermute | solution.py:19
  66.2 2.2 %collective-permute-start.1 = (bf16[256,256]{1,0:T(8,128)(2,1)}, bf16[256,256]{1,0:T(8,128)(2,1)S(1)}, u32[]{:S(2)}, u32[]{:S(2)}) collective-permute-start(bf16[256,256]{1,0:T(8,128)(2,1)} %pad_maximum_fusion.7), channel_id=1, source_target_pairs={{0,16},{16,0},{32,48},{48,32},{64,80},{80,64},{96,112},{112,96},{1... | collective-permute-start | bytes 393224 | tf_op jit(solution)/shard_map/ppermute | solution.py:19
  69.2 2.2 %fusion.66 = (bf16[512,128]{1,0:T(8,128)(2,1)S(1)}, bf16[512,128]{1,0:T(8,128)(2,1)S(1)}, bf16[512,128]{1,0:T(8,128)(2,1)S(1)}) fusion(bf16[512,2,128]{2,1,0:T(2,128)(2,1)S(1)} %bitcast.342, pred[2,128]{1,0:T(4,128)(4,1)S(1)} %get-tuple-element.220, bf16[512,2,128]{2,1,0:T(2,128)(2,1)S(1)} %bitcast.356, bf16[512,2,128]{2,1,0:T(2,128)(2,1)S(1)} %bitcast.350), kind=kLoop, calls=%fused_computation.94 | loop fusion | flops 589824 | bytes 1179904 | tf_op jit(solution)/shard_map/reduce_sum | solution.py:74
  72.2 3.1 %collective-permute-start = (bf16[512,256]{1,0:T(8,128)(2,1)}, bf16[512,256]{1,0:T(8,128)(2,1)}, u32[]{:S(2)}, u32[]{:S(2)}) collective-permute-start(bf16[512,256]{1,0:T(8,128)(2,1)} %pad_maximum_fusion.3), channel_id=1, source_target_pairs={{0,16},{16,0},{32,48},{48,32},{64,80},{80,64},{96,112},{112,96},{1... | collective-permute-start | bytes 786440 | tf_op jit(solution)/shard_map/ppermute | solution.py:19
  76.0 2.2 %collective-permute-start.10 = (bf16[32,256]{1,0:T(8,128)(2,1)S(1)}, bf16[32,256]{1,0:T(8,128)(2,1)S(1)}, u32[]{:S(2)}, u32[]{:S(2)}) collective-permute-start(bf16[32,256]{1,0:T(8,128)(2,1)S(1)} %get-tuple-element.207), channel_id=1, source_target_pairs={{0,16},{16,0},{32,48},{48,32},{64,80},{80,64},{96,112},{112,96},{1... | collective-permute-start | bytes 49160 | tf_op jit(solution)/shard_map/ppermute | solution.py:19
  78.1 6.7 %while.2 = (s32[]{:T(128)}, f32[2,512,128]{2,1,0:T(8,128)S(1)}, f32[2,512,2]{1,2,0:T(2,128)S(1)}, bf16[2,512,128]{2,1,0:T(8,128)(2,1)S(1)}, bf16[1024,128]{0,1:T...) while((s32[]{:T(128)}, f32[2,512,128]{2,1,0:T(8,128)S(1)}, f32[2,512,2]{1,2,0:T(2,128)S(1)}, ...), condition=%wide.region_3.4_spmd, body=%wide.region_0.3_spmd.sunk | while | flops 276888576 | bytes 16154749 | solution.py:46
  86.3 3.1 %collective-permute-start.6 = (bf16[64,256]{1,0:T(8,128)(2,1)S(1)}, bf16[64,256]{1,0:T(8,128)(2,1)S(1)}, u32[]{:S(2)}, u32[]{:S(2)}) collective-permute-start(bf16[64,256]{1,0:T(8,128)(2,1)S(1)} %get-tuple-element.199), channel_id=1, source_target_pairs={{0,16},{16,0},{32,48},{48,32},{64,80},{80,64},{96,112},{112,96},{1... | collective-permute-start | bytes 98312 | tf_op jit(solution)/shard_map/ppermute | solution.py:19
  89.5 4.4 %collective-permute-start.11 = (bf16[64,256]{1,0:T(8,128)(2,1)S(1)}, bf16[64,256]{1,0:T(8,128)(2,1)S(1)}, u32[]{:S(2)}, u32[]{:S(2)}) collective-permute-start(bf16[64,256]{1,0:T(8,128)(2,1)S(1)} %pad_maximum_fusion.15), channel_id=1, source_target_pairs={{0,32},{32,0},{16,48},{48,16},{64,96},{96,64},{80,112},{112,80},{1... | collective-permute-start | bytes 98312 | tf_op jit(solution)/shard_map/ppermute | solution.py:19
  94.5 2.4 %collective-permute-start.7 = (bf16[128,256]{1,0:T(8,128)(2,1)S(1)}, bf16[128,256]{1,0:T(8,128)(2,1)S(1)}, u32[]{:S(2)}, u32[]{:S(2)}) collective-permute-start(bf16[128,256]{1,0:T(8,128)(2,1)S(1)} %pad_maximum_fusion.12), channel_id=1, source_target_pairs={{0,32},{32,0},{16,48},{48,16},{64,96},{96,64},{80,112},{112,80},{1... | collective-permute-start | bytes 196616 | tf_op jit(solution)/shard_map/ppermute | solution.py:19
  97.0 3.2 %collective-permute-start.12 = (bf16[128,256]{1,0:T(8,128)(2,1)S(1)}, bf16[128,256]{1,0:T(8,128)(2,1)S(1)}, u32[]{:S(2)}, u32[]{:S(2)}) collective-permute-start(bf16[128,256]{1,0:T(8,128)(2,1)S(1)} %pad_maximum_fusion.13), channel_id=1, source_target_pairs={{0,64},{64,0},{16,80},{80,16},{32,96},{96,32},{48,112},{112,48},{1... | collective-permute-start | bytes 196616 | tf_op jit(solution)/shard_map/ppermute | solution.py:19
  100.8 4.4 %collective-permute-start.4 = (bf16[256,256]{1,0:T(8,128)(2,1)S(1)}, bf16[256,256]{1,0:T(8,128)(2,1)S(1)}, u32[]{:S(2)}, u32[]{:S(2)}) collective-permute-start(bf16[256,256]{1,0:T(8,128)(2,1)S(1)} %pad_maximum_fusion.8), channel_id=1, source_target_pairs={{0,32},{32,0},{16,48},{48,16},{64,96},{96,64},{80,112},{112,80},{1... | collective-permute-start | bytes 393224 | tf_op jit(solution)/shard_map/ppermute | solution.py:19
  105.2 2.1 %collective-permute-start.8 = (bf16[256,256]{1,0:T(8,128)(2,1)S(1)}, bf16[256,256]{1,0:T(8,128)(2,1)S(1)}, u32[]{:S(2)}, u32[]{:S(2)}) collective-permute-start(bf16[256,256]{1,0:T(8,128)(2,1)S(1)} %pad_maximum_fusion.9), channel_id=1, source_target_pairs={{0,64},{64,0},{16,80},{80,16},{32,96},{96,32},{48,112},{112,48},{1... | collective-permute-start | bytes 393224 | tf_op jit(solution)/shard_map/ppermute | solution.py:19
  108.1 4.2 %collective-permute-start.13 = (bf16[256,256]{1,0:T(8,128)(2,1)S(1)}, bf16[256,256]{1,0:T(8,128)(2,1)S(1)}, u32[]{:S(2)}, u32[]{:S(2)}) collective-permute-start(bf16[256,256]{1,0:T(8,128)(2,1)S(1)} %pad_maximum_fusion.10), channel_id=1, source_target_pairs={{0,128},{128,0},{16,144},{144,16},{32,160},{160,32},{48,176},{176,... | collective-permute-start | bytes 393224 | tf_op jit(solution)/shard_map/ppermute | solution.py:19
  113.7 2.4 %collective-permute-start.2 = (bf16[512,256]{1,0:T(8,128)(2,1)}, bf16[512,256]{1,0:T(8,128)(2,1)}, u32[]{:S(2)}, u32[]{:S(2)}) collective-permute-start(bf16[512,256]{1,0:T(8,128)(2,1)} %pad_maximum_fusion.4), channel_id=1, source_target_pairs={{0,32},{32,0},{16,48},{48,16},{64,96},{96,64},{80,112},{112,80},{1... | collective-permute-start | bytes 786440 | tf_op jit(solution)/shard_map/ppermute | solution.py:19
  116.9 3.2 %collective-permute-start.5 = (bf16[512,256]{1,0:T(8,128)(2,1)}, bf16[512,256]{1,0:T(8,128)(2,1)}, u32[]{:S(2)}, u32[]{:S(2)}) collective-permute-start(bf16[512,256]{1,0:T(8,128)(2,1)} %pad_maximum_fusion.5), channel_id=1, source_target_pairs={{0,64},{64,0},{16,80},{80,16},{32,96},{96,32},{48,112},{112,48},{1... | collective-permute-start | bytes 786440 | tf_op jit(solution)/shard_map/ppermute | solution.py:19
  120.8 2.0 %collective-permute-start.9 = (bf16[512,256]{1,0:T(8,128)(2,1)}, bf16[512,256]{1,0:T(8,128)(2,1)}, u32[]{:S(2)}, u32[]{:S(2)}) collective-permute-start(bf16[512,256]{1,0:T(8,128)(2,1)} %pad_maximum_fusion.6), channel_id=1, source_target_pairs={{0,128},{128,0},{16,144},{144,16},{32,160},{160,32},{48,176},{176,... | collective-permute-start | bytes 786440 | tf_op jit(solution)/shard_map/ppermute | solution.py:19
  123.6 6.7 %collective-permute-start.14 = (bf16[512,256]{1,0:T(8,128)(2,1)}, bf16[512,256]{1,0:T(8,128)(2,1)}, u32[]{:S(2)}, u32[]{:S(2)}) collective-permute-start(bf16[512,256]{1,0:T(8,128)(2,1)} %get-tuple-element.195), channel_id=1, source_target_pairs={{0,256},{256,0},{16,272},{272,16},{32,288},{288,32},{48,304},{304,... | collective-permute-start | bytes 786440 | tf_op jit(solution)/shard_map/ppermute | solution.py:19
  145.3 2.1 %collective-permute-done.9 = bf16[512,256]{1,0:T(8,128)(2,1)} collective-permute-done((bf16[512,256]{1,0:T(8,128)(2,1)}, bf16[512,256]{1,0:T(8,128)(2,1)}, u32[]{:S(2)}, u32[]{:S(2)}) %collective-permute-start.9) | collective-permute-done | bytes 262176 | tf_op jit(solution)/shard_map/ppermute | solution.py:19
  149.1 1.8 fusion.88
  154.5 1.7 constant_dynamic-update-slice_fusion.11
  156.1 1.8 fusion.89
  160.4 2.8 %fusion.37 = bf16[16,64,128]{2,1,0:T(8,128)(2,1)S(1)} fusion(f32[16,64,128]{2,1,0:T(8,128)S(1)} %copy.110, f32[16,64,128]{2,1,0:T(8,128)} %bitcast.383, f32[128]{0:T(128)S(1)} %copy-done.26, pred[128]{0:T(512)(128)(4,1)S(1)} %copy-done.27, f32[16,64,128]{2,1,0:T(8,128)S(1)} %bitcast.365, f32[16,64,128]{2,1,0:T(8,128)} %bitcast.363, ...), kind=kLoop, calls=%fused_computation.49 | loop fusion | flops 5636096 | bytes 6554240 | tf_op jit(solution)/shard_map/convert_element_type | solution.py:129
  163.2 16.6 %all_to_all.70 = bf16[16,64,128]{2,1,0:T(8,128)(2,1)S(1)} all-to-all(bf16[16,64,128]{2,1,0:T(8,128)(2,1)S(1)} %fusion.37), channel_id=1, replica_groups=mesh['seg'=32,'head'=16] {'head'}, dimensions={0} | all-to-all | bytes 524288 | tf_op jit(solution)/shard_map/all_to_all | solution.py:130
  (198 shorter events, 57.3 us)
Async XLA Ops:
  1.7 23.5 %all-to-all-start = ((bf16[64,16,128]{2,0,1:T(8,128)(2,1)}), bf16[64,16,128]{2,0,1:T(8,128)(2,1)S(1)}, u32[]{:S(2)}, u32[]{:S(2)}) async-start(bf16[64,16,128]{2,0,1:T(8,128)(2,1)} %copy_bitcast_fusion.3), calls=%async_computation | async-start | bytes 524288 | tf_op jit(solution)/shard_map/all_to_all | solution.py:55
  17.3 54.0 %copy-start.23 = (pred[2,128]{1,0:T(4,128)(4,1)}, pred[2,128]{1,0:T(4,128)(4,1)S(1)}, u32[]{:S(2)}) copy-start(pred[2,128]{1,0:T(4,128)(4,1)S(1)} %get-tuple-element.220) | copy-start | bytes 772
  22.1 49.2 %copy-start.21 = (pred[4,128]{1,0:T(4,128)(4,1)}, pred[4,128]{1,0:T(4,128)(4,1)S(1)}, u32[]{:S(2)}) copy-start(pred[4,128]{1,0:T(4,128)(4,1)S(1)} %get-tuple-element.222) | copy-start | bytes 1540
  25.3 17.5 %all-to-all-start.1 = ((bf16[64,16,128]{2,0,1:T(8,128)(2,1)}), bf16[64,16,128]{2,0,1:T(8,128)(2,1)S(1)}, u32[]{:S(2)}, u32[]{:S(2)}) async-start(bf16[64,16,128]{2,0,1:T(8,128)(2,1)} %copy_bitcast_fusion.2), calls=%async_computation.1 | async-start | bytes 524288 | tf_op jit(solution)/shard_map/all_to_all | solution.py:56
  32.8 42.5 %copy-start.18 = (pred[8,128]{1,0:T(8,128)(4,1)}, pred[8,128]{1,0:T(8,128)(4,1)S(1)}, u32[]{:S(2)}) copy-start(pred[8,128]{1,0:T(8,128)(4,1)S(1)} %get-tuple-element.224) | copy-start | bytes 3076
  42.8 14.6 %all-to-all-start.2 = ((bf16[64,16,128]{2,0,1:T(8,128)(2,1)}), bf16[64,16,128]{2,0,1:T(8,128)(2,1)S(1)}, u32[]{:S(2)}, u32[]{:S(2)}) async-start(bf16[64,16,128]{2,0,1:T(8,128)(2,1)} %copy_bitcast_fusion.1), calls=%async_computation.2 | async-start | bytes 524288 | tf_op jit(solution)/shard_map/all_to_all | solution.py:57
  48.2 11.2 %copy-start.15 = (pred[16,128]{1,0:T(8,128)(4,1)}, pred[16,128]{1,0:T(8,128)(4,1)S(1)}, u32[]{:S(2)}) copy-start(pred[16,128]{1,0:T(8,128)(4,1)S(1)} %get-tuple-element.226) | copy-start | bytes 6148
  48.8 20.4 %copy-start.12 = (pred[32,128]{1,0:T(8,128)(4,1)}, pred[32,128]{1,0:T(8,128)(4,1)S(1)}, u32[]{:S(2)}) copy-start(pred[32,128]{1,0:T(8,128)(4,1)S(1)} %get-tuple-element.228) | copy-start | bytes 12292
  57.6 39.3 %copy-start.7 = (bf16[32,128]{1,0:T(8,128)(2,1)}, bf16[32,128]{1,0:T(8,128)(2,1)S(1)}, u32[]{:S(2)}) copy-start(bf16[32,128]{1,0:T(8,128)(2,1)S(1)} %get-tuple-element.155) | copy-start | bytes 24580
  57.6 39.3 %copy-start.8 = (bf16[32,128]{1,0:T(8,128)(2,1)}, bf16[32,128]{1,0:T(8,128)(2,1)S(1)}, u32[]{:S(2)}) copy-start(bf16[32,128]{1,0:T(8,128)(2,1)S(1)} %get-tuple-element.156) | copy-start | bytes 24580
  60.6 40.3 %collective-permute-start.3 = (bf16[128,256]{1,0:T(8,128)(2,1)S(1)}, bf16[128,256]{1,0:T(8,128)(2,1)S(1)}, u32[]{:S(2)}, u32[]{:S(2)}) collective-permute-start(bf16[128,256]{1,0:T(8,128)(2,1)S(1)} %pad_maximum_fusion.11), channel_id=1, source_target_pairs={{0,16},{16,0},{32,48},{48,32},{64,80},{80,64},{96,112},{112,96},{1... | collective-permute-start | bytes 196616 | tf_op jit(solution)/shard_map/ppermute | solution.py:19
  66.2 46.8 %collective-permute-start.1 = (bf16[256,256]{1,0:T(8,128)(2,1)}, bf16[256,256]{1,0:T(8,128)(2,1)S(1)}, u32[]{:S(2)}, u32[]{:S(2)}) collective-permute-start(bf16[256,256]{1,0:T(8,128)(2,1)} %pad_maximum_fusion.7), channel_id=1, source_target_pairs={{0,16},{16,0},{32,48},{48,32},{64,80},{80,64},{96,112},{112,96},{1... | collective-permute-start | bytes 393224 | tf_op jit(solution)/shard_map/ppermute | solution.py:19
  72.2 58.1 %collective-permute-start = (bf16[512,256]{1,0:T(8,128)(2,1)}, bf16[512,256]{1,0:T(8,128)(2,1)}, u32[]{:S(2)}, u32[]{:S(2)}) collective-permute-start(bf16[512,256]{1,0:T(8,128)(2,1)} %pad_maximum_fusion.3), channel_id=1, source_target_pairs={{0,16},{16,0},{32,48},{48,32},{64,80},{80,64},{96,112},{112,96},{1... | collective-permute-start | bytes 786440 | tf_op jit(solution)/shard_map/ppermute | solution.py:19
  76.0 13.5 %collective-permute-start.10 = (bf16[32,256]{1,0:T(8,128)(2,1)S(1)}, bf16[32,256]{1,0:T(8,128)(2,1)S(1)}, u32[]{:S(2)}, u32[]{:S(2)}) collective-permute-start(bf16[32,256]{1,0:T(8,128)(2,1)S(1)} %get-tuple-element.207), channel_id=1, source_target_pairs={{0,16},{16,0},{32,48},{48,32},{64,80},{80,64},{96,112},{112,96},{1... | collective-permute-start | bytes 49160 | tf_op jit(solution)/shard_map/ppermute | solution.py:19
  86.3 8.1 %collective-permute-start.6 = (bf16[64,256]{1,0:T(8,128)(2,1)S(1)}, bf16[64,256]{1,0:T(8,128)(2,1)S(1)}, u32[]{:S(2)}, u32[]{:S(2)}) collective-permute-start(bf16[64,256]{1,0:T(8,128)(2,1)S(1)} %get-tuple-element.199), channel_id=1, source_target_pairs={{0,16},{16,0},{32,48},{48,32},{64,80},{80,64},{96,112},{112,96},{1... | collective-permute-start | bytes 98312 | tf_op jit(solution)/shard_map/ppermute | solution.py:19
  89.5 7.4 %collective-permute-start.11 = (bf16[64,256]{1,0:T(8,128)(2,1)S(1)}, bf16[64,256]{1,0:T(8,128)(2,1)S(1)}, u32[]{:S(2)}, u32[]{:S(2)}) collective-permute-start(bf16[64,256]{1,0:T(8,128)(2,1)S(1)} %pad_maximum_fusion.15), channel_id=1, source_target_pairs={{0,32},{32,0},{16,48},{48,16},{64,96},{96,64},{80,112},{112,80},{1... | collective-permute-start | bytes 98312 | tf_op jit(solution)/shard_map/ppermute | solution.py:19
  94.5 10.7 %collective-permute-start.7 = (bf16[128,256]{1,0:T(8,128)(2,1)S(1)}, bf16[128,256]{1,0:T(8,128)(2,1)S(1)}, u32[]{:S(2)}, u32[]{:S(2)}) collective-permute-start(bf16[128,256]{1,0:T(8,128)(2,1)S(1)} %pad_maximum_fusion.12), channel_id=1, source_target_pairs={{0,32},{32,0},{16,48},{48,16},{64,96},{96,64},{80,112},{112,80},{1... | collective-permute-start | bytes 196616 | tf_op jit(solution)/shard_map/ppermute | solution.py:19
  97.0 10.4 %collective-permute-start.12 = (bf16[128,256]{1,0:T(8,128)(2,1)S(1)}, bf16[128,256]{1,0:T(8,128)(2,1)S(1)}, u32[]{:S(2)}, u32[]{:S(2)}) collective-permute-start(bf16[128,256]{1,0:T(8,128)(2,1)S(1)} %pad_maximum_fusion.13), channel_id=1, source_target_pairs={{0,64},{64,0},{16,80},{80,16},{32,96},{96,32},{48,112},{112,48},{1... | collective-permute-start | bytes 196616 | tf_op jit(solution)/shard_map/ppermute | solution.py:19
  100.8 15.3 %collective-permute-start.4 = (bf16[256,256]{1,0:T(8,128)(2,1)S(1)}, bf16[256,256]{1,0:T(8,128)(2,1)S(1)}, u32[]{:S(2)}, u32[]{:S(2)}) collective-permute-start(bf16[256,256]{1,0:T(8,128)(2,1)S(1)} %pad_maximum_fusion.8), channel_id=1, source_target_pairs={{0,32},{32,0},{16,48},{48,16},{64,96},{96,64},{80,112},{112,80},{1... | collective-permute-start | bytes 393224 | tf_op jit(solution)/shard_map/ppermute | solution.py:19
  105.2 14.8 %collective-permute-start.8 = (bf16[256,256]{1,0:T(8,128)(2,1)S(1)}, bf16[256,256]{1,0:T(8,128)(2,1)S(1)}, u32[]{:S(2)}, u32[]{:S(2)}) collective-permute-start(bf16[256,256]{1,0:T(8,128)(2,1)S(1)} %pad_maximum_fusion.9), channel_id=1, source_target_pairs={{0,64},{64,0},{16,80},{80,16},{32,96},{96,32},{48,112},{112,48},{1... | collective-permute-start | bytes 393224 | tf_op jit(solution)/shard_map/ppermute | solution.py:19
  108.1 14.7 %collective-permute-start.13 = (bf16[256,256]{1,0:T(8,128)(2,1)S(1)}, bf16[256,256]{1,0:T(8,128)(2,1)S(1)}, u32[]{:S(2)}, u32[]{:S(2)}) collective-permute-start(bf16[256,256]{1,0:T(8,128)(2,1)S(1)} %pad_maximum_fusion.10), channel_id=1, source_target_pairs={{0,128},{128,0},{16,144},{144,16},{32,160},{160,32},{48,176},{176,... | collective-permute-start | bytes 393224 | tf_op jit(solution)/shard_map/ppermute | solution.py:19
  113.7 21.8 %collective-permute-start.2 = (bf16[512,256]{1,0:T(8,128)(2,1)}, bf16[512,256]{1,0:T(8,128)(2,1)}, u32[]{:S(2)}, u32[]{:S(2)}) collective-permute-start(bf16[512,256]{1,0:T(8,128)(2,1)} %pad_maximum_fusion.4), channel_id=1, source_target_pairs={{0,32},{32,0},{16,48},{48,16},{64,96},{96,64},{80,112},{112,80},{1... | collective-permute-start | bytes 786440 | tf_op jit(solution)/shard_map/ppermute | solution.py:19
  116.1 16.4 %copy-start.2 = (bf16[256,256]{1,0:T(8,128)(2,1)}, bf16[256,256]{1,0:T(8,128)(2,1)S(1)}, u32[]{:S(2)}) copy-start(bf16[256,256]{1,0:T(8,128)(2,1)S(1)} %collective-permute-done.4) | copy-start | bytes 393220
  116.9 22.1 %collective-permute-start.5 = (bf16[512,256]{1,0:T(8,128)(2,1)}, bf16[512,256]{1,0:T(8,128)(2,1)}, u32[]{:S(2)}, u32[]{:S(2)}) collective-permute-start(bf16[512,256]{1,0:T(8,128)(2,1)} %pad_maximum_fusion.5), channel_id=1, source_target_pairs={{0,64},{64,0},{16,80},{80,16},{32,96},{96,32},{48,112},{112,48},{1... | collective-permute-start | bytes 786440 | tf_op jit(solution)/shard_map/ppermute | solution.py:19
  120.8 26.6 %collective-permute-start.9 = (bf16[512,256]{1,0:T(8,128)(2,1)}, bf16[512,256]{1,0:T(8,128)(2,1)}, u32[]{:S(2)}, u32[]{:S(2)}) collective-permute-start(bf16[512,256]{1,0:T(8,128)(2,1)} %pad_maximum_fusion.6), channel_id=1, source_target_pairs={{0,128},{128,0},{16,144},{144,16},{32,160},{160,32},{48,176},{176,... | collective-permute-start | bytes 786440 | tf_op jit(solution)/shard_map/ppermute | solution.py:19
  122.8 10.7 %copy-start.1 = (bf16[1024,256]{1,0:T(8,128)(2,1)}, bf16[1024,256]{1,0:T(8,128)(2,1)S(1)}, u32[]{:S(2)}) copy-start(bf16[1024,256]{1,0:T(8,128)(2,1)S(1)} %constant_dynamic-update-slice_fusion.2) | copy-start | bytes 1572868
  123.6 30.9 %collective-permute-start.14 = (bf16[512,256]{1,0:T(8,128)(2,1)}, bf16[512,256]{1,0:T(8,128)(2,1)}, u32[]{:S(2)}, u32[]{:S(2)}) collective-permute-start(bf16[512,256]{1,0:T(8,128)(2,1)} %get-tuple-element.195), channel_id=1, source_target_pairs={{0,256},{256,0},{16,272},{272,16},{32,288},{288,32},{48,304},{304,... | collective-permute-start | bytes 786440 | tf_op jit(solution)/shard_map/ppermute | solution.py:19
  140.9 11.2 %copy-start.9 = (bf16[64,2,64]{2,1,0:T(2,128)(2,1)S(1)}, bf16[64,2,64]{2,1,0:T(2,128)(2,1)}, u32[]{:S(2)}) copy-start(bf16[64,2,64]{2,1,0:T(2,128)(2,1)} %reshape.592) | copy-start | bytes 49156
  143.5 9.8 %copy-start.14 = (f32[16,128]{1,0:T(8,128)S(1)}, f32[16,128]{1,0:T(8,128)}, u32[]{:S(2)}) copy-start(f32[16,128]{1,0:T(8,128)} %get-tuple-element.227) | copy-start | bytes 24580
  143.6 9.8 %copy-start.16 = (pred[16,128]{1,0:T(8,128)(4,1)S(1)}, pred[16,128]{1,0:T(8,128)(4,1)}, u32[]{:S(2)}) copy-start(pred[16,128]{1,0:T(8,128)(4,1)} %copy-done.15) | copy-start | bytes 6148
  145.3 12.8 %copy-start.11 = (bf16[32,2,64]{2,1,0:T(2,128)(2,1)S(1)}, bf16[32,2,64]{2,1,0:T(2,128)(2,1)}, u32[]{:S(2)}) copy-start(bf16[32,2,64]{2,1,0:T(2,128)(2,1)} %reshape.598) | copy-start | bytes 24580
  151.0 9.3 %copy-start.10 = (f32[32,128]{1,0:T(8,128)S(1)}, f32[32,128]{1,0:T(8,128)}, u32[]{:S(2)}) copy-start(f32[32,128]{1,0:T(8,128)} %get-tuple-element.229) | copy-start | bytes 49156
  (15 other events, 54.8 us)
where the time goes:
time: 182 us; the launch traced here: 181 us
  starting transfers between devices  69.7 us (38%)
  other arithmetic  33.1 us (18%)
  local copies, waits for them, and re-layouts  29.9 us (16%)
  waiting for transfers between devices  20.2 us (11%)
  blocking collectives  16.6 us (9%)
  matrix products  9.89 us (5%)
    ppermute x15, starting transfers between devices, from_partner(): return lax.ppermute(block, axis, route)  48.6 us
    all_to_all x1, blocking collectives, per_device(): lax.all_to_all(merged, 'head', split_axis=0, concat_axis=1, tiled=True)  16.6 us
    all_to_all x1, starting transfers between devices, per_device(): lax.all_to_all(queries, 'head', split_axis=1, concat_axis=0, tiled=True)  11.8 us
    all_to_all x1, waiting for transfers between devices, per_device(): lax.all_to_all(value_states, 'head', split_axis=1, concat_axis=0, tiled=T...  8.42 us
    all_to_all x1, waiting for transfers between devices, per_device(): lax.all_to_all(key_states, 'head', split_axis=1, concat_axis=0, tiled=True)  8.24 us
    gather x5, other arithmetic, column_mask(): offsets[:, level_id][column_head][None, :]  6.31 us
    concatenate x12, other arithmetic, per_device(): jnp.concatenate([current, from_partner(current, 'seg', bit_index)], axis=0)  5.95 us
    all_to_all x1, starting transfers between devices, per_device(): lax.all_to_all(key_states, 'head', split_axis=1, concat_axis=0, tiled=True)  5.81 us
  transfers between devices with their start and end apart: 18, of which 4 were waited for; matrix products, arithmetic and copies ran while one was open for 32% of the time, Pallas kernels for 0%

commit v1 on v0

v1 whole, which is shorter than its diff:
```python
import functools

import jax
import jax.numpy as jnp
from jax import lax
from jax.experimental import pallas as pl
from jax.experimental.pallas import tpu as pltpu
from jax.sharding import PartitionSpec as P

MESH = pl.DeviceIdType.MESH
BF = jnp.bfloat16
F32 = jnp.float32

ROWS = 64
BLOCK = 1024
WIDE = 128
HEADS = 16
NX, NY = 4, 8
Q_AT = {1: 0, 2: 512, 3: 768, 4: 896, 5: 960}
X_AT = {2: 0, 3: 256, 4: 384, 5: 448}
X_ROWS = 480


def rows_of(level):
    return BLOCK >> level


def remote(src, dst, send, recv, seg, head):
    return pltpu.make_async_remote_copy(
        src_ref=src, dst_ref=dst, send_sem=send, recv_sem=recv,
        device_id=(seg, head), device_id_type=MESH,
    )


def drain(ref, sem):
    pltpu.make_async_copy(ref, ref, sem).wait()


def low_lanes(rows):
    return lax.broadcasted_iota(jnp.int32, (rows, WIDE), 1) < WIDE // 2


def dot_t(a, b):
    return lax.dot_general(a, b, (((1,), (1,)), ((), ())), preferred_element_type=F32)


def dot(a, b):
    return lax.dot_general(a, b, (((1,), (0,)), ((), ())), preferred_element_type=F32)


def attend(q, k, v_low, v_high):
    rows = q.shape[0]
    low = low_lanes(rows)
    zero = jnp.zeros_like(q)
    q = q * jnp.asarray(0.125, BF)
    both = jnp.concatenate([jnp.where(low, q, zero), jnp.where(low, zero, q)], axis=0)
    scores = dot_t(both, k)
    top = jnp.max(scores, axis=1, keepdims=True)
    probs = jnp.exp(scores - top).astype(BF)
    first = dot(probs[:rows], v_low)
    second = dot(probs[rows:], v_high)
    total = jnp.where(low, first, second)
    denom = pltpu.roll(jnp.where(low, second, first), WIDE // 2, 1)
    return total, denom, jnp.where(low, top[:rows], top[rows:])


def with_ones(v):
    low = low_lanes(v.shape[0])
    one = jnp.ones_like(v)
    return jnp.where(low, v, one), jnp.where(low, one, v)


def kernel(
    off_ref, q_ref, k_ref, v_ref, out_ref,
    pick, full, own1, got1, gx, gy3, gy4, gy5, qsel, v_one,
    acc, den, top, acc_e, den_e, top_e, merged,
    in_recv, in_send, one_recv, one_send, x_recv, x_send, y_recv, y_send, out_recv, out_send,
):
    seg = lax.axis_index("seg")
    head = lax.axis_index("head")
    x = lax.rem(seg, NX)
    y = lax.div(seg, NX)

    barrier = pltpu.get_barrier_semaphore()

    def greet_head(i, carry):
        pl.semaphore_signal(barrier, inc=1, device_id=(seg, lax.rem(head + i, HEADS)), device_id_type=MESH)
        return carry

    def greet_x(i, carry):
        pl.semaphore_signal(barrier, inc=1, device_id=(y * NX + lax.rem(x + i, NX), head), device_id_type=MESH)
        return carry

    def greet_y(i, carry):
        pl.semaphore_signal(barrier, inc=1, device_id=(lax.rem(y + i, NY) * NX + x, head), device_id_type=MESH)
        return carry

    lax.fori_loop(1, HEADS, greet_head, 0)
    lax.fori_loop(1, NX, greet_x, 0)
    lax.fori_loop(1, NY, greet_y, 0)
    pl.semaphore_wait(barrier, (HEADS - 1) + (NX - 1) + (NY - 1))

    mine = pl.ds(pl.multiple_of(head * ROWS, ROWS), ROWS)
    my_columns = pl.ds(pl.multiple_of(head * WIDE, WIDE), WIDE)
    for a, ref in enumerate((k_ref, v_ref, q_ref)):
        pltpu.make_async_copy(ref.at[:, my_columns], full.at[a, mine], in_recv.at[a]).start()

        def send_in(i, carry, a=a, ref=ref):
            to = lax.rem(head + i, HEADS)
            columns = pl.ds(pl.multiple_of(to * WIDE, WIDE), WIDE)
            remote(ref.at[:, columns], full.at[a, mine], in_send.at[a], in_recv.at[a], seg, to).start()
            return carry

        lax.fori_loop(1, HEADS, send_in, 0)

    r = lax.broadcasted_iota(jnp.int32, (256, 256), 0)
    c = lax.broadcasted_iota(jnp.int32, (256, 256), 1)
    for h in range(2):
        src = jnp.full((256, 256), -1, jnp.int32)
        at = 248
        for level in range(5, 0, -1):
            at -= 256 >> level
            src = jnp.where(r < at + (256 >> level), ((r - at) << level) + off_ref[h, level], src)
        src = jnp.where(r < 248, src, -1)
        pick[h * 256:(h + 1) * 256] = jnp.where(c == src, 1.0, 0.0).astype(BF)

    def select(a):
        low = low_lanes(256)
        pieces = []
        for n in range(4):
            both = dot(pick[...], full[a, n * 256:(n + 1) * 256])
            pieces.append(jnp.where(low, both[:256], both[256:]))
        parts = {}
        at = 0
        for level in range(1, 6):
            step = 256 >> level
            parts[level] = jnp.concatenate([piece[at:at + step] for piece in pieces], axis=0).astype(BF)
            at += step
        return parts

    partner_x = y * NX + (x + 1 - 2 * lax.rem(x, 2))
    partner_y = (y + 1 - 2 * lax.rem(y, 2)) * NX + x

    def start_x(kv):
        parts = select(kv)
        own1[kv] = parts[1]
        for level in range(2, 6):
            gx[kv, x, X_AT[level]:X_AT[level] + rows_of(level)] = parts[level]
        remote(own1.at[kv], got1.at[kv], one_send.at[kv], one_recv.at[kv], partner_x, head).start()

        def send_x(i, carry):
            to = y * NX + lax.rem(x + i, NX)
            remote(gx.at[kv, x], gx.at[kv, x], x_send.at[kv], x_recv.at[kv], to, head).start()
            return carry

        lax.fori_loop(1, NX, send_x, 0)

    def start_y(kv):
        drain(gx.at[kv, pl.ds(0, NX - 1)], x_recv.at[kv])
        for level in range(3, 6):
            rows = rows_of(level)
            src = gx.at[kv, :, pl.ds(X_AT[level], rows)]
            send, recv = y_send.at[level - 3, kv], y_recv.at[level - 3, kv]
            if level == 3:
                remote(src, gy3.at[kv], send, recv, partner_y, head).start()
            else:
                group = 1 << (level - 2)
                base = y - lax.rem(y, group)
                held = gy4 if level == 4 else gy5

                def send_y(i, carry):
                    to = base + lax.rem(y + i, group)
                    remote(src, held.at[kv, group - 1 - i], send, recv, to * NX + x, head).start()
                    return carry

                lax.fori_loop(1, group, send_y, 0)

    drain(full.at[0], in_recv.at[0])
    start_x(0)
    drain(full.at[1], in_recv.at[1])
    start_x(1)
    v_one[0], v_one[1] = with_ones(full[1])
    start_y(0)
    start_y(1)

    drain(full.at[2], in_recv.at[2])
    parts = select(2)
    for level in range(1, 6):
        qsel[Q_AT[level]:Q_AT[level] + rows_of(level)] = parts[level]

    def level_zero(i, carry):
        rows = pl.ds(pl.multiple_of(i * 128, 128), 128)
        acc[rows], den[rows], top[rows] = attend(full[2, rows], full[0], v_one[0], v_one[1])
        return carry

    lax.fori_loop(0, 8, level_zero, 0)

    def keys(level, kv):
        if level == 1:
            return jnp.concatenate([own1[kv], got1[kv]], axis=0)
        rows = rows_of(level)
        near = gx[kv, :, X_AT[level]:X_AT[level] + rows, :].reshape(NX * rows, WIDE)
        if level == 2:
            return near
        far = {3: gy3, 4: gy4, 5: gy5}[level][kv].reshape(BLOCK - NX * rows, WIDE)
        return jnp.concatenate([near, far], axis=0)

    for level in range(1, 6):
        for kv in range(2):
            if level == 1:
                drain(got1.at[kv], one_recv.at[kv])
            elif level >= 3:
                drain({3: gy3, 4: gy4, 5: gy5}[level].at[kv], y_recv.at[level - 3, kv])
        rows, stride = rows_of(level), 1 << level
        k = keys(level, 0)
        v_low, v_high = with_ones(keys(level, 1))
        step = min(rows, 128)
        for n in range(rows // step):
            at = Q_AT[level] + n * step
            found = attend(qsel[at:at + step], k, v_low, v_high)
            for held, value in zip((acc_e, den_e, top_e), found):
                for o in range(stride):
                    held[pl.ds(n * step * stride + o, step, stride=stride), :] = value

        lanes = low_lanes(128)
        offset = jnp.where(lanes, off_ref[0, level], off_ref[1, level])

        def merge(i, carry):
            part = pl.ds(pl.multiple_of(i * 128, 128), 128)
            t = lax.broadcasted_iota(jnp.int32, (128, WIDE), 0)
            chosen = (t & (stride - 1)) == offset
            level_top = jnp.where(chosen, top_e[part], -jnp.inf)
            old = top[part]
            new = jnp.maximum(old, level_top)
            fade, weight = jnp.exp(old - new), jnp.exp(level_top - new)
            acc[part] = acc[part] * fade + weight * acc_e[part]
            den[part] = den[part] * fade + weight * den_e[part]
            top[part] = new
            return carry

        lax.fori_loop(0, 8, merge, 0)

    def finish(i, carry):
        part = pl.ds(pl.multiple_of(i * 128, 128), 128)
        merged[part] = (acc[part] / den[part]).astype(BF)
        return carry

    lax.fori_loop(0, 8, finish, 0)
    pltpu.make_async_copy(merged.at[mine], out_ref.at[:, my_columns], out_recv).start()

    def send_out(i, carry):
        to = lax.rem(head + i, HEADS)
        part = pl.ds(pl.multiple_of(to * ROWS, ROWS), ROWS)
        remote(merged.at[part], out_ref.at[:, my_columns], out_send, out_recv, seg, to).start()
        return carry

    lax.fori_loop(1, HEADS, send_out, 0)

    others = pl.ds(0, BLOCK - ROWS)
    for a in range(3):
        drain(full.at[a, others], in_send.at[a])
    for kv in range(2):
        drain(own1.at[kv], one_send.at[kv])
        drain(gx.at[kv, pl.ds(0, NX - 1)], x_send.at[kv])
        for n, held in enumerate((gy3, gy4, gy5)):
            drain(held.at[kv], y_send.at[n, kv])
    drain(merged.at[others], out_send)
    drain(out_ref, out_recv)


def per_device(queries, key_states, value_states, offsets):
    dma = pltpu.SemaphoreType.DMA
    anywhere = pl.BlockSpec(memory_space=pl.ANY)
    return pl.pallas_call(
        kernel,
        out_shape=jax.ShapeDtypeStruct(queries.shape, BF),
        in_specs=[pl.BlockSpec(memory_space=pltpu.SMEM)] + [anywhere] * 3,
        out_specs=anywhere,
        scratch_shapes=[
            pltpu.VMEM((512, 256), BF),
            pltpu.VMEM((3, BLOCK, WIDE), BF),
            pltpu.VMEM((2, 512, WIDE), BF),
            pltpu.VMEM((2, 512, WIDE), BF),
            pltpu.VMEM((2, NX, X_ROWS, WIDE), BF),
            pltpu.VMEM((2, NX, 128, WIDE), BF),
            pltpu.VMEM((2, 3, NX, 64, WIDE), BF),
            pltpu.VMEM((2, 7, NX, 32, WIDE), BF),
            pltpu.VMEM((992, WIDE), BF),
            pltpu.VMEM((2, BLOCK, WIDE), BF),
        ] + [pltpu.VMEM((BLOCK, WIDE), F32)] * 6 + [
            pltpu.VMEM((BLOCK, WIDE), BF),
            dma((3,)), dma((3,)), dma((2,)), dma((2,)), dma((2,)), dma((2,)),
            dma((3, 2)), dma((3, 2)), dma, dma,
        ],
        compiler_params=pltpu.CompilerParams(
            collective_id=0, has_side_effects=True, vmem_limit_bytes=48 * 1024 * 1024
        ),
        cost_estimate=pl.CostEstimate(flops=1100000000, bytes_accessed=1100000, transcendentals=4200000),
    )(offsets, queries, key_states, value_states)


def solution(mesh):
    rows = P(("seg", "head"), None)
    return jax.shard_map(
        per_device, mesh=mesh, in_specs=(rows, rows, rows, P("head", None)), out_specs=rows, check_vma=False
    )
```

time: 182 us -> 79.1 us (0.43)
  Pallas kernels: 0 us -> 74.6 us
  starting transfers between devices: 69.7 us -> 0 us
  other arithmetic: 33.1 us -> 0 us
  local copies, waits for them, and re-layouts: 29.9 us -> 4.23 us
  waiting for transfers between devices: 20.2 us -> 0 us
  blocking collectives: 16.6 us -> 0 us
  matrix products: 9.89 us -> 0 us
    pallas_call x0 -> x1, Pallas kernels: none -> 74.6 us  [per_device(): pl.pallas_call(kernel, out_shape=jax.ShapeDtypeStruct(queries.shape, BF),...]
    ppermute x15 -> x0, starting transfers between devices: 48.6 us -> none  [from_partner(): return lax.ppermute(block, axis, route)]
    all_to_all x3 -> x0, starting transfers between devices: 21.1 us -> none  [the longest x1 11.8 us: per_device(): lax.all_to_all(queries, 'head', split_axis=1, concat_axis=0, tiled=True)]
    all_to_all x3 -> x0, waiting for transfers between devices: 18.1 us -> none  [the longest x1 8.42 us: per_device(): lax.all_to_all(value_states, 'head', split_axis=1, concat_axis=0, tiled=T...]
    all_to_all x1 -> x0, blocking collectives: 16.6 us -> none  [per_device(): lax.all_to_all(merged, 'head', split_axis=0, concat_axis=1, tiled=True)]
    dot_general x14 -> x0, matrix products: 9.89 us -> none  [the longest x7 5.11 us: attend_block(): jnp.einsum('hqk,khe->qhe', probs, value_view, preferred_element_type=jnp....]
    slice x15 -> x0, local copies, waits for them, and re-layouts: 8.64 us -> none  [the longest x10 5.08 us: attend_packed(): gathered[:, :width]]
    reduce_sum x12 -> x0, other arithmetic: 8.36 us -> none  [the longest x5 4.34 us: pick_rows(): jnp.sum(jnp.where(mask[None], shaped, jnp.zeros_like(shaped)), axis=1)]
  transfers between devices with their start and end apart: 18 -> 0, of which waited for: 4 -> 0; matrix products, arithmetic and copies ran while one was open for 32% -> 0% of each run, Pallas kernels for 0% -> 0%
where the time goes in v1:
time: 79.1 us; the launch traced here: 78.9 us
  Pallas kernels  74.6 us (94%)
  local copies, waits for them, and re-layouts  4.23 us (5%)
    pallas_call x1, Pallas kernels, per_device(): pl.pallas_call(kernel, out_shape=jax.ShapeDtypeStruct(queries.shape, BF),...  74.6 us
    unnamed x9, local copies, waits for them, and re-layouts  4.23 us

profile of v1, /device:TPU:1, one launch (start us, length us, event | category | flops | bytes accessed | tf_op | source)
XLA Modules:
  0.0 78.9 jit_solution(205911806841477380)
XLA Ops:
  0.0 0.0 copy-start
  0.0 0.9 %copy-done = bf16[64,2048]{1,0:T(8,128)(2,1)S(1)} copy-done((bf16[64,2048]{1,0:T(8,128)(2,1)S(1)}, bf16[64,2048]{1,0:T(8,128)(2,1)}, u32[]{:S(2)}) %copy-start) | copy-done | bytes 262168
  1.0 0.0 copy-start.1
  1.0 0.9 %copy-done.1 = bf16[64,2048]{1,0:T(8,128)(2,1)S(1)} copy-done((bf16[64,2048]{1,0:T(8,128)(2,1)S(1)}, bf16[64,2048]{1,0:T(8,128)(2,1)}, u32[]{:S(2)}) %copy-start.1) | copy-done | bytes 262168
  1.9 0.0 copy-start.2
  1.9 0.9 %copy-done.2 = bf16[64,2048]{1,0:T(8,128)(2,1)S(1)} copy-done((bf16[64,2048]{1,0:T(8,128)(2,1)S(1)}, bf16[64,2048]{1,0:T(8,128)(2,1)}, u32[]{:S(2)}) %copy-start.2) | copy-done | bytes 262168
  2.9 0.0 copy-start.3
  2.9 0.7 copy-done.3
  3.5 74.6 %shard_map.46 = bf16[64,2048]{1,0:T(8,128)(2,1)S(1)} custom-call(s32[2,6]{1,0:T(2,128)S(1)} %copy-done.3, bf16[64,2048]{1,0:T(8,128)(2,1)S(1)} %copy-done, bf16[64,2048]{1,0:T(8,128)(2,1)S(1)} %copy-done.1, bf16[64,2048]{1,0:T(8,128)(2,1)S(1)} %copy-done.2), custom_call_target="tpu_custom_call" | custom-call | flops 1100000000 | bytes 1100000 | tf_op jit(solution)/shard_map/pallas_call | solution.py:274
  78.2 0.7 copy.6
Async XLA Ops:
  0.0 0.9 %copy-start = (bf16[64,2048]{1,0:T(8,128)(2,1)S(1)}, bf16[64,2048]{1,0:T(8,128)(2,1)}, u32[]{:S(2)}) copy-start(bf16[64,2048]{1,0:T(8,128)(2,1)} %q_ref.1) | copy-start | bytes 786436
  1.0 0.9 %copy-start.1 = (bf16[64,2048]{1,0:T(8,128)(2,1)S(1)}, bf16[64,2048]{1,0:T(8,128)(2,1)}, u32[]{:S(2)}) copy-start(bf16[64,2048]{1,0:T(8,128)(2,1)} %k_ref.1) | copy-start | bytes 786436
  1.9 0.9 %copy-start.2 = (bf16[64,2048]{1,0:T(8,128)(2,1)S(1)}, bf16[64,2048]{1,0:T(8,128)(2,1)}, u32[]{:S(2)}) copy-start(bf16[64,2048]{1,0:T(8,128)(2,1)} %v_ref.1) | copy-start | bytes 786436
  2.9 0.7 copy-start.3

commit v2 on v1

v2 whole, which is shorter than its diff:
```python
import jax
import jax.numpy as jnp
from jax import lax
from jax.experimental import pallas as pl
from jax.experimental.pallas import tpu as pltpu
from jax.sharding import PartitionSpec as P

MESH = pl.DeviceIdType.MESH
BF = jnp.bfloat16
F32 = jnp.float32

ROWS = 64
BLOCK = 1024
WIDE = 128
HEADS = 16
NX, NY = 4, 8
Q_AT = {1: 0, 2: 512, 3: 768, 4: 896, 5: 960}
UP_AT = {3: 0, 4: 128, 5: 192}
UP_ROWS = 224
COLUMN_KEYS = 256
STAT_ROWS = 32
STAT_GROUPS = UP_ROWS // STAT_ROWS


def rows_of(level):
    return BLOCK >> level


def remote(src, dst, send, recv, seg, head):
    return pltpu.make_async_remote_copy(
        src_ref=src, dst_ref=dst, send_sem=send, recv_sem=recv,
        device_id=(seg, head), device_id_type=MESH,
    )


def drain(ref, sem):
    pltpu.make_async_copy(ref, ref, sem).wait()


def lanes_of(rows):
    return lax.broadcasted_iota(jnp.int32, (rows, WIDE), 1)


def low_lanes(rows):
    return lanes_of(rows) < WIDE // 2


def dot_t(a, b):
    return lax.dot_general(a, b, (((1,), (1,)), ((), ())), preferred_element_type=F32)


def dot(a, b):
    return lax.dot_general(a, b, (((1,), (0,)), ((), ())), preferred_element_type=F32)


def attend(q, k, v_low, v_high):
    rows = q.shape[0]
    low = low_lanes(rows)
    zero = jnp.zeros_like(q)
    q = q * jnp.asarray(0.125, BF)
    both = jnp.concatenate([jnp.where(low, q, zero), jnp.where(low, zero, q)], axis=0)
    scores = dot_t(both, k)
    top = jnp.max(scores, axis=1, keepdims=True)
    probs = jnp.exp(scores - top).astype(BF)
    first = dot(probs[:rows], v_low)
    second = dot(probs[rows:], v_high)
    total = jnp.where(low, first, second)
    denom = pltpu.roll(jnp.where(low, second, first), WIDE // 2, 1)
    return total, denom, jnp.where(low, top[:rows], top[rows:])


def with_ones(v):
    low = low_lanes(v.shape[0])
    one = jnp.ones_like(v)
    return jnp.where(low, v, one), jnp.where(low, one, v)


def kernel(
    off_hbm, q_ref, k_ref, v_ref, out_ref,
    off_ref, pick, full, own1, got1, gx, yk, qsel, qx, part_o, part_s, back_o, back_s, v_one,
    acc, den, top, acc_e, den_e, top_e, merged,
    off_sem, in_recv, in_send, one_recv, one_send, x_recv, x_send, y_recv, y_send,
    q_recv, q_send, back_recv, back_send, out_recv, out_send,
):
    seg = lax.axis_index("seg")
    head = lax.axis_index("head")
    x = lax.rem(seg, NX)
    y = lax.div(seg, NX)
    offsets = pltpu.make_async_copy(off_hbm, off_ref, off_sem)
    offsets.start()

    barrier = pltpu.get_barrier_semaphore()

    def at_x(i):
        return y * NX + lax.rem(x + i, NX)

    def greet_head(i, carry):
        pl.semaphore_signal(barrier, inc=1, device_id=(seg, lax.rem(head + i, HEADS)), device_id_type=MESH)
        return carry

    def greet_x(i, carry):
        pl.semaphore_signal(barrier, inc=1, device_id=(at_x(i), head), device_id_type=MESH)
        return carry

    def greet_y(i, carry):
        pl.semaphore_signal(barrier, inc=1, device_id=(lax.rem(y + i, NY) * NX + x, head), device_id_type=MESH)
        return carry

    lax.fori_loop(1, HEADS, greet_head, 0)
    lax.fori_loop(1, NX, greet_x, 0)
    lax.fori_loop(1, NY, greet_y, 0)
    pl.semaphore_wait(barrier, (HEADS - 1) + (NX - 1) + (NY - 1))

    mine = pl.ds(pl.multiple_of(head * ROWS, ROWS), ROWS)
    others = pl.ds(0, BLOCK - ROWS)
    my_columns = pl.ds(pl.multiple_of(head * WIDE, WIDE), WIDE)

    def exchange(a):
        ref = (k_ref, v_ref, q_ref)[a]

        def send_in(i, carry):
            to = lax.rem(head + i, HEADS)
            columns = pl.ds(pl.multiple_of(to * WIDE, WIDE), WIDE)
            remote(ref.at[:, columns], full.at[a, mine], in_send.at[a], in_recv.at[a], seg, to).start()
            return carry

        lax.fori_loop(1, HEADS, send_in, 0)
        pltpu.make_async_copy(ref.at[:, my_columns], full.at[a, mine], in_recv.at[a]).start()

    exchange(0)

    offsets.wait()
    r = lax.broadcasted_iota(jnp.int32, (256, 256), 0)
    c = lax.broadcasted_iota(jnp.int32, (256, 256), 1)
    for h in range(2):
        src = jnp.full((256, 256), -1, jnp.int32)
        at = 248
        for level in range(5, 0, -1):
            at -= 256 >> level
            src = jnp.where(r < at + (256 >> level), ((r - at) << level) + off_ref[h, level], src)
        src = jnp.where(r < 248, src, -1)
        pick[h * 256:(h + 1) * 256] = jnp.where(c == src, 1.0, 0.0).astype(BF)

    def select(a):
        low = low_lanes(256)
        pieces = []
        for n in range(4):
            both = dot(pick[...], full[a, n * 256:(n + 1) * 256])
            pieces.append(jnp.where(low, both[:256], both[256:]))
        parts = {}
        at = 0
        for level in range(1, 6):
            step = 256 >> level
            parts[level] = jnp.concatenate([piece[at:at + step] for piece in pieces], axis=0).astype(BF)
            at += step
        return parts

    partner_x = y * NX + (x + 1 - 2 * lax.rem(x, 2))

    def start_levels(kv):
        parts = select(kv)
        for level in range(3, 6):
            group = 1 << (level - 2)
            rows = rows_of(level)
            place = lax.rem(y, group)
            slot = yk.at[kv, level - 3, pl.ds(pl.multiple_of(place * rows, rows), rows)]
            slot[...] = parts[level]

            def send_y(i, carry):
                to = y - place + lax.rem(place + i, group)
                remote(slot, slot, y_send.at[kv, level - 3], y_recv.at[kv, level - 3], to * NX + x, head).start()
                return carry

            lax.fori_loop(1, group, send_y, 0)
        own1[kv] = parts[1]
        gx[kv, x] = parts[2]
        remote(own1.at[kv], got1.at[kv], one_send.at[kv], one_recv.at[kv], partner_x, head).start()

        def send_x(i, carry):
            remote(gx.at[kv, x], gx.at[kv, x], x_send.at[kv], x_recv.at[kv], at_x(i), head).start()
            return carry

        lax.fori_loop(1, NX, send_x, 0)

    drain(full.at[0, others], in_send.at[0])
    exchange(1)
    drain(full.at[0], in_recv.at[0])
    start_levels(0)
    drain(full.at[1, others], in_send.at[1])
    exchange(2)
    drain(full.at[1], in_recv.at[1])
    start_levels(1)
    v_one[0], v_one[1] = with_ones(full[1])

    drain(full.at[2], in_recv.at[2])
    parts = select(2)
    for level in range(3, 6):
        qx[x, UP_AT[level]:UP_AT[level] + rows_of(level)] = parts[level]

    def send_q(i, carry):
        remote(qx.at[x], qx.at[x], q_send, q_recv, at_x(i), head).start()
        return carry

    lax.fori_loop(1, NX, send_q, 0)
    for level in range(1, 3):
        qsel[Q_AT[level]:Q_AT[level] + rows_of(level)] = parts[level]

    def level_zero(i, carry):
        rows = pl.ds(pl.multiple_of(i * 128, 128), 128)
        acc[rows], den[rows], top[rows] = attend(full[2, rows], full[0], v_one[0], v_one[1])
        return carry

    lax.fori_loop(0, 8, level_zero, 0)

    drain(qx.at[pl.ds(0, NX - 1)], q_recv)
    group_lane = lax.rem(lanes_of(STAT_ROWS), WIDE // 2) // 8
    stats = [jnp.zeros((STAT_ROWS, WIDE), F32) for _ in range(NX)]
    for level in range(3, 6):
        rows = rows_of(level)
        for kv in range(2):
            drain(yk.at[kv, level - 3, pl.ds(0, COLUMN_KEYS - rows)], y_recv.at[kv, level - 3])
        at = UP_AT[level]
        v_low, v_high = with_ones(yk[1, level - 3])
        for n in range(NX):
            total, denom, peak = attend(qx[n, at:at + rows], yk[0, level - 3], v_low, v_high)
            part_o[n, at:at + rows] = (total / denom).astype(BF)
            lse = peak + jnp.log(denom)
            for m in range(rows // STAT_ROWS):
                stats[n] = jnp.where(
                    group_lane == at // STAT_ROWS + m, lse[m * STAT_ROWS:(m + 1) * STAT_ROWS], stats[n]
                )
    for n in range(NX):
        part_s[n] = stats[n]
    back_o[x] = part_o[x]
    back_s[x] = part_s[x]

    def send_back(i, carry):
        to = lax.rem(x + i, NX)
        remote(part_o.at[to], back_o.at[x], back_send.at[0], back_recv.at[0], at_x(i), head).start()
        remote(part_s.at[to], back_s.at[x], back_send.at[1], back_recv.at[1], at_x(i), head).start()
        return carry

    lax.fori_loop(1, NX, send_back, 0)

    def spread(at, stride, values):
        for held, value in zip((acc_e, den_e, top_e), values):
            for o in range(stride):
                held[pl.ds(at * stride + o, value.shape[0], stride=stride), :] = value

    def merge_level(level):
        stride = 1 << level
        offset = jnp.where(low_lanes(128), off_ref[0, level], off_ref[1, level])

        def merge(i, carry):
            part = pl.ds(pl.multiple_of(i * 128, 128), 128)
            t = lax.broadcasted_iota(jnp.int32, (128, WIDE), 0)
            chosen = (t & (stride - 1)) == offset
            level_top = jnp.where(chosen, top_e[part], -jnp.inf)
            old = top[part]
            new = jnp.maximum(old, level_top)
            fade, weight = jnp.exp(old - new), jnp.exp(level_top - new)
            acc[part] = acc[part] * fade + weight * acc_e[part]
            den[part] = den[part] * fade + weight * den_e[part]
            top[part] = new
            return carry

        lax.fori_loop(0, 8, merge, 0)

    for level in range(1, 3):
        for kv in range(2):
            if level == 1:
                drain(got1.at[kv], one_recv.at[kv])
            else:
                drain(gx.at[kv, pl.ds(0, NX - 1)], x_recv.at[kv])
        if level == 1:
            k, v = (jnp.concatenate([own1[kv], got1[kv]], axis=0) for kv in range(2))
        else:
            k, v = (gx[kv].reshape(BLOCK, WIDE) for kv in range(2))
        v_low, v_high = with_ones(v)
        for n in range(rows_of(level) // 128):
            at = Q_AT[level] + n * 128
            spread(n * 128, 1 << level, attend(qsel[at:at + 128], k, v_low, v_high))
        merge_level(level)

    drain(back_o.at[pl.ds(0, NX - 1)], back_recv.at[0])
    drain(back_s.at[pl.ds(0, NX - 1)], back_recv.at[1])
    low = low_lanes(STAT_ROWS)
    for level in range(3, 6):
        for m in range(rows_of(level) // STAT_ROWS):
            at = UP_AT[level] + m * STAT_ROWS
            lses = []
            for n in range(NX):
                here = jnp.where(group_lane == at // STAT_ROWS, back_s[n], -jnp.inf)
                lses.append(jnp.where(
                    low,
                    jnp.max(jnp.where(low, here, -jnp.inf), axis=1, keepdims=True),
                    jnp.max(jnp.where(low, -jnp.inf, here), axis=1, keepdims=True),
                ))
            peak = jnp.maximum(jnp.maximum(lses[0], lses[1]), jnp.maximum(lses[2], lses[3]))
            weights = [jnp.exp(lse - peak) for lse in lses]
            total = sum(w * back_o[n, at:at + STAT_ROWS].astype(F32) for n, w in enumerate(weights))
            spread(m * STAT_ROWS, 1 << level, (total, sum(weights), peak))
        merge_level(level)

    def finish(i, carry):
        part = pl.ds(pl.multiple_of(i * 128, 128), 128)
        merged[part] = (acc[part] / den[part]).astype(BF)
        return carry

    lax.fori_loop(0, 8, finish, 0)

    def send_out(i, carry):
        to = lax.rem(head + i, HEADS)
        part = pl.ds(pl.multiple_of(to * ROWS, ROWS), ROWS)
        remote(merged.at[part], out_ref.at[:, my_columns], out_send, out_recv, seg, to).start()
        return carry

    lax.fori_loop(1, HEADS, send_out, 0)
    pltpu.make_async_copy(merged.at[mine], out_ref.at[:, my_columns], out_recv).start()

    drain(full.at[2, others], in_send.at[2])
    for kv in range(2):
        drain(own1.at[kv], one_send.at[kv])
        drain(gx.at[kv, pl.ds(0, NX - 1)], x_send.at[kv])
        for level in range(3, 6):
            drain(yk.at[kv, level - 3, pl.ds(0, COLUMN_KEYS - rows_of(level))], y_send.at[kv, level - 3])
    drain(qx.at[pl.ds(0, NX - 1)], q_send)
    drain(back_o.at[pl.ds(0, NX - 1)], back_send.at[0])
    drain(back_s.at[pl.ds(0, NX - 1)], back_send.at[1])
    drain(merged.at[others], out_send)
    drain(out_ref, out_recv)


def per_device(queries, key_states, value_states, offsets):
    dma = pltpu.SemaphoreType.DMA
    hbm = pl.BlockSpec(memory_space=pltpu.HBM)
    return pl.pallas_call(
        kernel,
        out_shape=jax.ShapeDtypeStruct(queries.shape, BF),
        in_specs=[hbm] * 4,
        out_specs=pl.BlockSpec(memory_space=pl.ANY),
        scratch_shapes=[
            pltpu.SMEM((2, 6), jnp.int32),
            pltpu.VMEM((512, 256), BF),
            pltpu.VMEM((3, BLOCK, WIDE), BF),
            pltpu.VMEM((2, 512, WIDE), BF),
            pltpu.VMEM((2, 512, WIDE), BF),
            pltpu.VMEM((2, NX, 256, WIDE), BF),
            pltpu.VMEM((2, 3, COLUMN_KEYS, WIDE), BF),
            pltpu.VMEM((768, WIDE), BF),
            pltpu.VMEM((NX, UP_ROWS, WIDE), BF),
            pltpu.VMEM((NX, UP_ROWS, WIDE), BF),
            pltpu.VMEM((NX, STAT_ROWS, WIDE), F32),
            pltpu.VMEM((NX, UP_ROWS, WIDE), BF),
            pltpu.VMEM((NX, STAT_ROWS, WIDE), F32),
            pltpu.VMEM((2, BLOCK, WIDE), BF),
        ] + [pltpu.VMEM((BLOCK, WIDE), F32)] * 6 + [
            pltpu.VMEM((BLOCK, WIDE), BF),
            dma, dma((3,)), dma((3,)), dma((2,)), dma((2,)), dma((2,)), dma((2,)), dma((2, 3)), dma((2, 3)),
            dma, dma, dma((2,)), dma((2,)), dma, dma,
        ],
        compiler_params=pltpu.CompilerParams(
            collective_id=0, has_side_effects=True, vmem_limit_bytes=48 * 1024 * 1024
        ),
        cost_estimate=pl.CostEstimate(flops=1100000000, bytes_accessed=1100000, transcendentals=4200000),
    )(*(pltpu.with_memory_space_constraint(a, pltpu.HBM) for a in (offsets, queries, key_states, value_states)))


def solution(mesh):
    rows = P(("seg", "head"), None)
    return jax.shard_map(
        per_device, mesh=mesh, in_specs=(rows, rows, rows, P("head", None)), out_specs=rows, check_vma=False
    )
```

time: 79.1 us -> 60.9 us (0.77)
  Pallas kernels: 74.6 us -> 60.1 us
  local copies, waits for them, and re-layouts: 4.23 us -> 0.71 us
    pallas_call x1, Pallas kernels: 74.6 us -> 60.1 us  [per_device(): pl.pallas_call(kernel, out_shape=jax.ShapeDtypeStruct(queries.shape, BF),...]
    unnamed x9 -> x1, local copies, waits for them, and re-layouts: 4.23 us -> 0.71 us
where the time goes in v2:
time: 60.9 us; the launch traced here: 60.8 us
  Pallas kernels  60.1 us (99%)
  local copies, waits for them, and re-layouts  0.71 us (1%)
    pallas_call x1, Pallas kernels, per_device(): pl.pallas_call(kernel, out_shape=jax.ShapeDtypeStruct(queries.shape, BF),...  60.1 us

profile of v2, /device:TPU:1, one launch (start us, length us, event | category | flops | bytes accessed | tf_op | source)
XLA Modules:
  0.0 60.8 jit_solution(11280863021789897741)
XLA Ops:
  0.0 60.1 %shard_map.46 = bf16[64,2048]{1,0:T(8,128)(2,1)S(1)} custom-call(s32[2,6]{1,0:T(2,128)} %off_hbm.1, bf16[64,2048]{1,0:T(8,128)(2,1)} %q_ref.1, bf16[64,2048]{1,0:T(8,128)(2,1)} %k_ref.1, bf16[64,2048]{1,0:T(8,128)(2,1)} %v_ref.1), custom_call_target="tpu_custom_call" | custom-call | flops 1100000000 | bytes 1100000 | tf_op jit(solution)/shard_map/pallas_call | solution.py:337
  60.1 0.7 %copy.6 = bf16[64,2048]{1,0:T(8,128)(2,1)} copy(bf16[64,2048]{1,0:T(8,128)(2,1)S(1)} %shard_map.46) | data formatting | bytes 524288

commit v3 on v2

--- a/solution.py
+++ b/solution.py
@@ -13,6 +13,7 @@
 BLOCK = 1024
 WIDE = 128
 HEADS = 16
+D = 2048
 NX, NY = 4, 8
 Q_AT = {1: 0, 2: 512, 3: 768, 4: 896, 5: 960}
 UP_AT = {3: 0, 4: 128, 5: 192}
@@ -77,10 +78,10 @@
 
 def kernel(
     off_hbm, q_ref, k_ref, v_ref, out_ref,
-    off_ref, pick, full, own1, got1, gx, yk, qsel, qx, part_o, part_s, back_o, back_s, v_one,
-    acc, den, top, acc_e, den_e, top_e, merged,
-    off_sem, in_recv, in_send, one_recv, one_send, x_recv, x_send, y_recv, y_send,
-    q_recv, q_send, back_recv, back_send, out_recv, out_send,
+    off_ref, off_tiles, pick, pick_up, full, own1, got1, gx, yk, qsel, qx, part_o, part_s, back_o, back_s, v_one,
+    acc, den, top, acc_e, den_e, top_e, up_o, up_d, up_t, merged, final, early, late, late_in, placed,
+    off_sem, off_recv, off_send, in_recv, in_send, one_recv, one_send, x_recv, x_send, y_recv, y_send,
+    q_recv, q_send, back_recv, back_send, early_recv, early_send, late_recv, late_send, out_sem,
 ):
     seg = lax.axis_index("seg")
     head = lax.axis_index("head")
@@ -130,6 +131,19 @@
     exchange(0)
 
     offsets.wait()
+    level_row = lax.broadcasted_iota(jnp.int32, (8, WIDE), 0)
+    tile = jnp.zeros((8, WIDE), jnp.int32)
+    for level in range(1, 6):
+        tile = jnp.where(level_row == level, jnp.where(low_lanes(8), off_ref[0, level], off_ref[1, level]), tile)
+    off_tiles[head] = tile
+
+    def send_offsets(i, carry):
+        to = lax.rem(head + i, HEADS)
+        remote(off_tiles.at[head], off_tiles.at[head], off_send, off_recv, seg, to).start()
+        return carry
+
+    lax.fori_loop(1, HEADS, send_offsets, 0)
+
     r = lax.broadcasted_iota(jnp.int32, (256, 256), 0)
     c = lax.broadcasted_iota(jnp.int32, (256, 256), 1)
     for h in range(2):
@@ -140,6 +154,16 @@
             src = jnp.where(r < at + (256 >> level), ((r - at) << level) + off_ref[h, level], src)
         src = jnp.where(r < 248, src, -1)
         pick[h * 256:(h + 1) * 256] = jnp.where(c == src, 1.0, 0.0).astype(BF)
+
+    r = lax.broadcasted_iota(jnp.int32, (64, 256), 0)
+    c = lax.broadcasted_iota(jnp.int32, (64, 256), 1)
+    for h in range(2):
+        j = r & 15
+        src = jnp.where(
+            j < 8, (j << 3) + off_ref[h, 3],
+            jnp.where(j < 12, ((j - 8) << 4) + off_ref[h, 4], ((j - 12) << 5) + off_ref[h, 5]),
+        ) + ((r >> 4) << 6)
+        pick_up[h * 64:(h + 1) * 64] = jnp.where((c == src) & (j < 14), 1.0, 0.0).astype(BF)
 
     def select(a):
         low = low_lanes(256)
@@ -282,41 +306,102 @@
             spread(n * 128, 1 << level, attend(qsel[at:at + 128], k, v_low, v_high))
         merge_level(level)
 
+    def finish(i, carry):
+        part = pl.ds(pl.multiple_of(i * 128, 128), 128)
+        merged[part] = (acc[part] / den[part]).astype(BF)
+        return carry
+
+    lax.fori_loop(0, 8, finish, 0)
+
+    def send_early(i, carry):
+        to = lax.rem(head + i, HEADS)
+        part = pl.ds(pl.multiple_of(to * ROWS, ROWS), ROWS)
+        remote(merged.at[part], early.at[:, my_columns], early_send, early_recv, seg, to).start()
+        return carry
+
+    lax.fori_loop(1, HEADS, send_early, 0)
+    pltpu.make_async_copy(merged.at[mine], early.at[:, my_columns], early_recv).start()
+
     drain(back_o.at[pl.ds(0, NX - 1)], back_recv.at[0])
     drain(back_s.at[pl.ds(0, NX - 1)], back_recv.at[1])
     low = low_lanes(STAT_ROWS)
-    for level in range(3, 6):
-        for m in range(rows_of(level) // STAT_ROWS):
-            at = UP_AT[level] + m * STAT_ROWS
-            lses = []
-            for n in range(NX):
-                here = jnp.where(group_lane == at // STAT_ROWS, back_s[n], -jnp.inf)
-                lses.append(jnp.where(
-                    low,
-                    jnp.max(jnp.where(low, here, -jnp.inf), axis=1, keepdims=True),
-                    jnp.max(jnp.where(low, -jnp.inf, here), axis=1, keepdims=True),
-                ))
-            peak = jnp.maximum(jnp.maximum(lses[0], lses[1]), jnp.maximum(lses[2], lses[3]))
-            weights = [jnp.exp(lse - peak) for lse in lses]
-            total = sum(w * back_o[n, at:at + STAT_ROWS].astype(F32) for n, w in enumerate(weights))
-            spread(m * STAT_ROWS, 1 << level, (total, sum(weights), peak))
-        merge_level(level)
-
-    def finish(i, carry):
-        part = pl.ds(pl.multiple_of(i * 128, 128), 128)
-        merged[part] = (acc[part] / den[part]).astype(BF)
-        return carry
-
-    lax.fori_loop(0, 8, finish, 0)
-
-    def send_out(i, carry):
+    for m in range(STAT_GROUPS):
+        rows = pl.ds(m * STAT_ROWS, STAT_ROWS)
+        lses = []
+        for n in range(NX):
+            here = jnp.where(group_lane == m, back_s[n], -jnp.inf)
+            lses.append(jnp.where(
+                low,
+                jnp.max(jnp.where(low, here, -jnp.inf), axis=1, keepdims=True),
+                jnp.max(jnp.where(low, -jnp.inf, here), axis=1, keepdims=True),
+            ))
+        peak = jnp.maximum(jnp.maximum(lses[0], lses[1]), jnp.maximum(lses[2], lses[3]))
+        weights = [jnp.exp(lse - peak) for lse in lses]
+        up_o[rows] = sum(w * back_o[n, rows].astype(F32) for n, w in enumerate(weights))
+        up_d[rows] = sum(weights)
+        up_t[rows] = peak
+
+    def merge_up(i, carry):
+        held = []
+        for level in range(3, 6):
+            count = 256 >> level
+            at = pl.ds(pl.multiple_of(UP_AT[level] + i * count, 8), count)
+            held.append((level, up_o[at], up_d[at], up_t[at]))
+        t = lax.broadcasted_iota(jnp.int32, (32, WIDE), 0)
+        for n in range(8):
+            part = pl.ds(pl.multiple_of(i * 256 + n * 32, 32), 32)
+            total, denom, peak = acc[part], den[part], top[part]
+            for level, *compact in held:
+                stride = 1 << level
+                count = 32 >> level
+                o, d, p = (
+                    jnp.concatenate([
+                        jnp.broadcast_to(v[n * count + k:n * count + k + 1], (stride, WIDE)) for k in range(count)
+                    ], axis=0) for v in compact
+                )
+                chosen = (t & (stride - 1)) == jnp.where(low_lanes(32), off_ref[0, level], off_ref[1, level])
+                p = jnp.where(chosen, p, -jnp.inf)
+                new = jnp.maximum(peak, p)
+                fade, weight = jnp.exp(peak - new), jnp.exp(p - new)
+                total = total * fade + weight * o
+                denom = denom * fade + weight * d
+                peak = new
+            final[part] = (total / denom).astype(BF)
+        part = pl.ds(pl.multiple_of(i * 256, 256), 256)
+        both = dot(pick_up[...], final[part])
+        rows = jnp.where(low_lanes(64), both[:64], both[64:]).astype(BF)
+        late[pl.ds(i * 4, 4)] = rows.reshape(4, 16, WIDE)
+        return carry
+
+    lax.fori_loop(0, 4, merge_up, 0)
+
+    def send_late(i, carry):
         to = lax.rem(head + i, HEADS)
-        part = pl.ds(pl.multiple_of(to * ROWS, ROWS), ROWS)
-        remote(merged.at[part], out_ref.at[:, my_columns], out_send, out_recv, seg, to).start()
-        return carry
-
-    lax.fori_loop(1, HEADS, send_out, 0)
-    pltpu.make_async_copy(merged.at[mine], out_ref.at[:, my_columns], out_recv).start()
+        remote(late.at[to], late_in.at[head], late_send, late_recv, seg, to).start()
+        return carry
+
+    lax.fori_loop(1, HEADS, send_late, 0)
+    late_in[head] = late[head]
+
+    drain(off_tiles.at[pl.ds(0, HEADS - 1)], off_recv)
+    drain(early, early_recv)
+    drain(late_in.at[pl.ds(0, HEADS - 1)], late_recv)
+    t = lax.broadcasted_iota(jnp.int32, (ROWS, WIDE), 0)
+    for n in range(HEADS):
+        columns = slice(n * WIDE, (n + 1) * WIDE)
+        value = early[:, columns].astype(F32)
+        rows = late_in[n].astype(F32)
+        at = 0
+        for level in range(3, 6):
+            stride = 1 << level
+            count = ROWS >> level
+            wide = jnp.concatenate(
+                [jnp.broadcast_to(rows[at + k:at + k + 1], (stride, WIDE)) for k in range(count)], axis=0
+            )
+            value = jnp.where((t & (stride - 1)) == off_tiles[n, level:level + 1], wide, value)
+            at += count
+        placed[:, columns] = value.astype(BF)
+    pltpu.make_async_copy(placed, out_ref, out_sem).start()
 
     drain(full.at[2, others], in_send.at[2])
     for kv in range(2):
@@ -327,8 +412,10 @@
     drain(qx.at[pl.ds(0, NX - 1)], q_send)
     drain(back_o.at[pl.ds(0, NX - 1)], back_send.at[0])
     drain(back_s.at[pl.ds(0, NX - 1)], back_send.at[1])
-    drain(merged.at[others], out_send)
-    drain(out_ref, out_recv)
+    drain(off_tiles.at[pl.ds(0, HEADS - 1)], off_send)
+    drain(merged.at[others], early_send)
+    drain(late.at[pl.ds(0, HEADS - 1)], late_send)
+    drain(out_ref, out_sem)
 
 
 def per_device(queries, key_states, value_states, offsets):
@@ -341,7 +428,9 @@
         out_specs=pl.BlockSpec(memory_space=pl.ANY),
         scratch_shapes=[
             pltpu.SMEM((2, 6), jnp.int32),
+            pltpu.VMEM((HEADS, 8, WIDE), jnp.int32),
             pltpu.VMEM((512, 256), BF),
+            pltpu.VMEM((128, 256), BF),
             pltpu.VMEM((3, BLOCK, WIDE), BF),
             pltpu.VMEM((2, 512, WIDE), BF),
             pltpu.VMEM((2, 512, WIDE), BF),
@@ -354,10 +443,15 @@
             pltpu.VMEM((NX, UP_ROWS, WIDE), BF),
             pltpu.VMEM((NX, STAT_ROWS, WIDE), F32),
             pltpu.VMEM((2, BLOCK, WIDE), BF),
-        ] + [pltpu.VMEM((BLOCK, WIDE), F32)] * 6 + [
+        ] + [pltpu.VMEM((BLOCK, WIDE), F32)] * 6 + [pltpu.VMEM((UP_ROWS, WIDE), F32)] * 3 + [
             pltpu.VMEM((BLOCK, WIDE), BF),
-            dma, dma((3,)), dma((3,)), dma((2,)), dma((2,)), dma((2,)), dma((2,)), dma((2, 3)), dma((2, 3)),
-            dma, dma, dma((2,)), dma((2,)), dma, dma,
+            pltpu.VMEM((BLOCK, WIDE), BF),
+            pltpu.VMEM((ROWS, D), BF),
+            pltpu.VMEM((HEADS, 16, WIDE), BF),
+            pltpu.VMEM((HEADS, 16, WIDE), BF),
+            pltpu.VMEM((ROWS, D), BF),
+            dma, dma, dma, dma((3,)), dma((3,)), dma((2,)), dma((2,)), dma((2,)), dma((2,)), dma((2, 3)), dma((2, 3)),
+            dma, dma, dma((2,)), dma((2,)), dma, dma, dma, dma, dma,
         ],
         compiler_params=pltpu.CompilerParams(
             collective_id=0, has_side_effects=True, vmem_limit_bytes=48 * 1024 * 1024

time: 60.9 us -> 60.3 us (level)
    pallas_call x1, Pallas kernels: 60.1 us -> 59.5 us  [per_device(): pl.pallas_call(kernel, out_shape=jax.ShapeDtypeStruct(queries.shape, BF),...]
where the time goes in v3:
time: 60.3 us; the launch traced here: 60.2 us
  Pallas kernels  59.5 us (99%)
  local copies, waits for them, and re-layouts  0.71 us (1%)
    pallas_call x1, Pallas kernels, per_device(): pl.pallas_call(kernel, out_shape=jax.ShapeDtypeStruct(queries.shape, BF),...  59.5 us

profile of v3, /device:TPU:1, one launch (start us, length us, event | category | flops | bytes accessed | tf_op | source)
XLA Modules:
  0.0 60.2 jit_solution(15431300009198412177)
XLA Ops:
  0.0 59.5 %shard_map.46 = bf16[64,2048]{1,0:T(8,128)(2,1)S(1)} custom-call(s32[2,6]{1,0:T(2,128)} %off_hbm.1, bf16[64,2048]{1,0:T(8,128)(2,1)} %q_ref.1, bf16[64,2048]{1,0:T(8,128)(2,1)} %k_ref.1, bf16[64,2048]{1,0:T(8,128)(2,1)} %v_ref.1), custom_call_target="tpu_custom_call" | custom-call | flops 1100000000 | bytes 1100000 | tf_op jit(solution)/shard_map/pallas_call | solution.py:424
  59.5 0.7 %copy.6 = bf16[64,2048]{1,0:T(8,128)(2,1)} copy(bf16[64,2048]{1,0:T(8,128)(2,1)S(1)} %shard_map.46) | data formatting | bytes 524288

commit v4 on v2

--- a/solution.py
+++ b/solution.py
@@ -13,6 +13,7 @@
 BLOCK = 1024
 WIDE = 128
 HEADS = 16
+D = 2048
 NX, NY = 4, 8
 Q_AT = {1: 0, 2: 512, 3: 768, 4: 896, 5: 960}
 UP_AT = {3: 0, 4: 128, 5: 192}
@@ -77,9 +78,9 @@
 
 def kernel(
     off_hbm, q_ref, k_ref, v_ref, out_ref,
-    off_ref, pick, full, own1, got1, gx, yk, qsel, qx, part_o, part_s, back_o, back_s, v_one,
-    acc, den, top, acc_e, den_e, top_e, merged,
-    off_sem, in_recv, in_send, one_recv, one_send, x_recv, x_send, y_recv, y_send,
+    off_ref, off_tiles, q_here, gather_up, up_out, up_in, pick, full, own1, got1, gx, yk, qsel, qx, part_o, part_s, back_o, back_s, v_one,
+    acc, den, top, acc_e, den_e, top_e, up_o, up_d, up_t, merged,
+    off_sem, q_sem, off_recv, off_send, up_recv, up_send, in_recv, in_send, one_recv, one_send, x_recv, x_send, y_recv, y_send,
     q_recv, q_send, back_recv, back_send, out_recv, out_send,
 ):
     seg = lax.axis_index("seg")
@@ -88,6 +89,8 @@
     y = lax.div(seg, NX)
     offsets = pltpu.make_async_copy(off_hbm, off_ref, off_sem)
     offsets.start()
+    queries_here = pltpu.make_async_copy(q_ref, q_here, q_sem)
+    queries_here.start()
 
     barrier = pltpu.get_barrier_semaphore()
 
@@ -127,9 +130,21 @@
         lax.fori_loop(1, HEADS, send_in, 0)
         pltpu.make_async_copy(ref.at[:, my_columns], full.at[a, mine], in_recv.at[a]).start()
 
+    offsets.wait()
+    level_row = lax.broadcasted_iota(jnp.int32, (4, WIDE), 0) + 3
+    tile = jnp.zeros((4, WIDE), jnp.int32)
+    for level in range(3, 6):
+        tile = jnp.where(level_row == level, jnp.where(low_lanes(4), off_ref[0, level], off_ref[1, level]), tile)
+    off_tiles[head] = tile
+
+    def send_offsets(i, carry):
+        to = lax.rem(head + i, HEADS)
+        remote(off_tiles.at[head], off_tiles.at[head], off_send, off_recv, seg, to).start()
+        return carry
+
+    lax.fori_loop(1, HEADS, send_offsets, 0)
     exchange(0)
 
-    offsets.wait()
     r = lax.broadcasted_iota(jnp.int32, (256, 256), 0)
     c = lax.broadcasted_iota(jnp.int32, (256, 256), 1)
     for h in range(2):
@@ -141,24 +156,53 @@
         src = jnp.where(r < 248, src, -1)
         pick[h * 256:(h + 1) * 256] = jnp.where(c == src, 1.0, 0.0).astype(BF)
 
-    def select(a):
-        low = low_lanes(256)
+    r = lax.broadcasted_iota(jnp.int32, (16, 3 * ROWS), 0)
+    c = lax.broadcasted_iota(jnp.int32, (16, 3 * ROWS), 1)
+    t = c & (ROWS - 1)
+    row = jnp.where(c < ROWS, t >> 3, jnp.where(c < 2 * ROWS, 8 + (t >> 4), 12 + (t >> 5)))
+    add_up = jnp.where(r == row, 1.0, 0.0).astype(BF)
+    r = lax.broadcasted_iota(jnp.int32, (UP_ROWS, HEADS * 16), 0)
+    c = lax.broadcasted_iota(jnp.int32, (UP_ROWS, HEADS * 16), 1)
+    r4, r5 = r - UP_AT[4], r - UP_AT[5]
+    src = jnp.where(
+        r < UP_AT[4], ((r >> 3) << 4) + (r & 7),
+        jnp.where(r < UP_AT[5], ((r4 >> 2) << 4) + 8 + (r4 & 3), ((r5 >> 1) << 4) + 12 + (r5 & 1)),
+    )
+    gather_up[...] = jnp.where(c == src, 1.0, 0.0).astype(BF)
+
+    queries_here.wait()
+    drain(off_tiles.at[pl.ds(0, HEADS - 1)], off_recv)
+    t = lax.broadcasted_iota(jnp.int32, (ROWS, WIDE), 0)
+    for n in range(HEADS):
+        value = q_here[:, n * WIDE:(n + 1) * WIDE].astype(F32)
+        kept = [
+            jnp.where((t & ((1 << level) - 1)) == off_tiles[n, level - 3:level - 2], value, 0.0)
+            for level in range(3, 6)
+        ]
+        up_out[n] = dot(add_up, jnp.concatenate(kept, axis=0).astype(BF)).astype(BF)
+
+    def select(a, last):
+        count = 256 - (256 >> last) if last < 5 else 256
+        low = low_lanes(count)
+        chosen = jnp.concatenate([pick[:count], pick[256:256 + count]], axis=0)
         pieces = []
         for n in range(4):
-            both = dot(pick[...], full[a, n * 256:(n + 1) * 256])
-            pieces.append(jnp.where(low, both[:256], both[256:]))
+            both = dot(chosen, full[a, n * 256:(n + 1) * 256])
+            pieces.append(jnp.where(low, both[:count], both[count:]))
         parts = {}
         at = 0
-        for level in range(1, 6):
+        for level in range(1, last + 1):
             step = 256 >> level
             parts[level] = jnp.concatenate([piece[at:at + step] for piece in pieces], axis=0).astype(BF)
             at += step
         return parts
 
-    partner_x = y * NX + (x + 1 - 2 * lax.rem(x, 2))
+    pair = x + 1 - 2 * lax.rem(x, 2)
+    partner_x = y * NX + pair
+    beside_x = at_x(NX - 1 + 2 * lax.rem(x, 2))
 
     def start_levels(kv):
-        parts = select(kv)
+        parts = select(kv, 5)
         for level in range(3, 6):
             group = 1 << (level - 2)
             rows = rows_of(level)
@@ -174,43 +218,44 @@
             lax.fori_loop(1, group, send_y, 0)
         own1[kv] = parts[1]
         gx[kv, x] = parts[2]
+        held = gx.at[kv, x]
+        remote(held, held, x_send.at[kv, 0], x_recv.at[kv, 0], partner_x, head).start()
+        remote(held, held, x_send.at[kv, 1], x_recv.at[kv, 1], beside_x, head).start()
         remote(own1.at[kv], got1.at[kv], one_send.at[kv], one_recv.at[kv], partner_x, head).start()
 
-        def send_x(i, carry):
-            remote(gx.at[kv, x], gx.at[kv, x], x_send.at[kv], x_recv.at[kv], at_x(i), head).start()
-            return carry
-
-        lax.fori_loop(1, NX, send_x, 0)
+    def pass_on(kv):
+        held = gx.at[kv, pair]
+        drain(held, x_recv.at[kv, 0])
+        remote(held, held, x_send.at[kv, 2], x_recv.at[kv, 2], beside_x, head).start()
 
     drain(full.at[0, others], in_send.at[0])
+
+    def send_up(i, carry):
+        to = lax.rem(head + i, HEADS)
+        remote(up_out.at[to], up_in.at[head], up_send, up_recv, seg, to).start()
+        return carry
+
+    lax.fori_loop(1, HEADS, send_up, 0)
+    up_in[head] = up_out[head]
     exchange(1)
     drain(full.at[0], in_recv.at[0])
     start_levels(0)
+
+    drain(up_in.at[pl.ds(0, HEADS - 1)], up_recv)
+    qx[x] = dot(gather_up[...], up_in[...].reshape(HEADS * 16, WIDE)).astype(BF)
+
+    def send_q(i, carry):
+        remote(qx.at[x], qx.at[x], q_send, q_recv, at_x(i), head).start()
+        return carry
+
+    lax.fori_loop(1, NX, send_q, 0)
+    pass_on(0)
     drain(full.at[1, others], in_send.at[1])
     exchange(2)
     drain(full.at[1], in_recv.at[1])
     start_levels(1)
     v_one[0], v_one[1] = with_ones(full[1])
-
-    drain(full.at[2], in_recv.at[2])
-    parts = select(2)
-    for level in range(3, 6):
-        qx[x, UP_AT[level]:UP_AT[level] + rows_of(level)] = parts[level]
-
-    def send_q(i, carry):
-        remote(qx.at[x], qx.at[x], q_send, q_recv, at_x(i), head).start()
-        return carry
-
-    lax.fori_loop(1, NX, send_q, 0)
-    for level in range(1, 3):
-        qsel[Q_AT[level]:Q_AT[level] + rows_of(level)] = parts[level]
-
-    def level_zero(i, carry):
-        rows = pl.ds(pl.multiple_of(i * 128, 128), 128)
-        acc[rows], den[rows], top[rows] = attend(full[2, rows], full[0], v_one[0], v_one[1])
-        return carry
-
-    lax.fori_loop(0, 8, level_zero, 0)
+    pass_on(1)
 
     drain(qx.at[pl.ds(0, NX - 1)], q_recv)
     group_lane = lax.rem(lanes_of(STAT_ROWS), WIDE // 2) // 8
@@ -242,91 +287,110 @@
 
     lax.fori_loop(1, NX, send_back, 0)
 
-    def spread(at, stride, values):
-        for held, value in zip((acc_e, den_e, top_e), values):
-            for o in range(stride):
-                held[pl.ds(at * stride + o, value.shape[0], stride=stride), :] = value
-
-    def merge_level(level):
-        stride = 1 << level
-        offset = jnp.where(low_lanes(128), off_ref[0, level], off_ref[1, level])
-
-        def merge(i, carry):
-            part = pl.ds(pl.multiple_of(i * 128, 128), 128)
-            t = lax.broadcasted_iota(jnp.int32, (128, WIDE), 0)
-            chosen = (t & (stride - 1)) == offset
-            level_top = jnp.where(chosen, top_e[part], -jnp.inf)
-            old = top[part]
-            new = jnp.maximum(old, level_top)
-            fade, weight = jnp.exp(old - new), jnp.exp(level_top - new)
-            acc[part] = acc[part] * fade + weight * acc_e[part]
-            den[part] = den[part] * fade + weight * den_e[part]
-            top[part] = new
-            return carry
-
-        lax.fori_loop(0, 8, merge, 0)
+    drain(full.at[2], in_recv.at[2])
+    parts = select(2, 2)
+    for level in range(1, 3):
+        qsel[Q_AT[level]:Q_AT[level] + rows_of(level)] = parts[level]
+    acc[...], den[...], top[...] = attend(full[2], full[0], v_one[0], v_one[1])
 
     for level in range(1, 3):
         for kv in range(2):
             if level == 1:
                 drain(got1.at[kv], one_recv.at[kv])
             else:
-                drain(gx.at[kv, pl.ds(0, NX - 1)], x_recv.at[kv])
+                drain(gx.at[kv, 0], x_recv.at[kv, 1])
+                drain(gx.at[kv, 0], x_recv.at[kv, 2])
         if level == 1:
             k, v = (jnp.concatenate([own1[kv], got1[kv]], axis=0) for kv in range(2))
         else:
             k, v = (gx[kv].reshape(BLOCK, WIDE) for kv in range(2))
         v_low, v_high = with_ones(v)
-        for n in range(rows_of(level) // 128):
-            at = Q_AT[level] + n * 128
-            spread(n * 128, 1 << level, attend(qsel[at:at + 128], k, v_low, v_high))
-        merge_level(level)
+        found = attend(qsel[Q_AT[level]:Q_AT[level] + rows_of(level)], k, v_low, v_high)
+        stride = 1 << level
+        for held, value in zip((acc_e, den_e, top_e), found):
+            for o in range(stride):
+                held[level - 1, pl.ds(o, rows_of(level), stride=stride), :] = value
 
     drain(back_o.at[pl.ds(0, NX - 1)], back_recv.at[0])
     drain(back_s.at[pl.ds(0, NX - 1)], back_recv.at[1])
     low = low_lanes(STAT_ROWS)
-    for level in range(3, 6):
-        for m in range(rows_of(level) // STAT_ROWS):
-            at = UP_AT[level] + m * STAT_ROWS
-            lses = []
-            for n in range(NX):
-                here = jnp.where(group_lane == at // STAT_ROWS, back_s[n], -jnp.inf)
-                lses.append(jnp.where(
-                    low,
-                    jnp.max(jnp.where(low, here, -jnp.inf), axis=1, keepdims=True),
-                    jnp.max(jnp.where(low, -jnp.inf, here), axis=1, keepdims=True),
-                ))
-            peak = jnp.maximum(jnp.maximum(lses[0], lses[1]), jnp.maximum(lses[2], lses[3]))
-            weights = [jnp.exp(lse - peak) for lse in lses]
-            total = sum(w * back_o[n, at:at + STAT_ROWS].astype(F32) for n, w in enumerate(weights))
-            spread(m * STAT_ROWS, 1 << level, (total, sum(weights), peak))
-        merge_level(level)
-
-    def finish(i, carry):
-        part = pl.ds(pl.multiple_of(i * 128, 128), 128)
-        merged[part] = (acc[part] / den[part]).astype(BF)
-        return carry
-
-    lax.fori_loop(0, 8, finish, 0)
-
-    def send_out(i, carry):
-        to = lax.rem(head + i, HEADS)
-        part = pl.ds(pl.multiple_of(to * ROWS, ROWS), ROWS)
-        remote(merged.at[part], out_ref.at[:, my_columns], out_send, out_recv, seg, to).start()
-        return carry
-
-    lax.fori_loop(1, HEADS, send_out, 0)
+    for m in range(STAT_GROUPS):
+        rows = pl.ds(m * STAT_ROWS, STAT_ROWS)
+        lses = []
+        for n in range(NX):
+            here = jnp.where(group_lane == m, back_s[n], -jnp.inf)
+            lses.append(jnp.where(
+                low,
+                jnp.max(jnp.where(low, here, -jnp.inf), axis=1, keepdims=True),
+                jnp.max(jnp.where(low, -jnp.inf, here), axis=1, keepdims=True),
+            ))
+        peak = jnp.maximum(jnp.maximum(lses[0], lses[1]), jnp.maximum(lses[2], lses[3]))
+        weights = [jnp.exp(lse - peak) for lse in lses]
+        up_o[rows] = sum(w * back_o[n, rows].astype(F32) for n, w in enumerate(weights))
+        up_d[rows] = sum(weights)
+        up_t[rows] = peak
+
+    def chosen_rows(rows, level):
+        t = lax.broadcasted_iota(jnp.int32, (rows, WIDE), 0)
+        return (t & ((1 << level) - 1)) == jnp.where(low_lanes(rows), off_ref[0, level], off_ref[1, level])
+
+    def merge(i, carry):
+        quarter = lax.rem(lax.div(head, 4) + i, 4)
+        held = {}
+        for level in range(3, 6):
+            count = 256 >> level
+            at = pl.ds(pl.multiple_of(UP_AT[level] + quarter * count, 8), count)
+            held[level] = (up_o[at], up_d[at], up_t[at])
+        for n in range(8):
+            part = pl.ds(pl.multiple_of(quarter * 256 + n * 32, 32), 32)
+            total, denom, peak = acc[part], den[part], top[part]
+            for level in range(1, 6):
+                if level < 3:
+                    o, d, p = (e[level - 1, part] for e in (acc_e, den_e, top_e))
+                else:
+                    count = 32 >> level
+                    o, d, p = (
+                        jnp.concatenate([
+                            jnp.broadcast_to(v[n * count + k:n * count + k + 1], (1 << level, WIDE))
+                            for k in range(count)
+                        ], axis=0) for v in held[level]
+                    )
+                p = jnp.where(chosen_rows(32, level), p, -jnp.inf)
+                new = jnp.maximum(peak, p)
+                fade, weight = jnp.exp(peak - new), jnp.exp(p - new)
+                total = total * fade + weight * o
+                denom = denom * fade + weight * d
+                peak = new
+            merged[part] = (total / denom).astype(BF)
+
+        def send_out(k, carry):
+            to = quarter * 4 + k
+
+            @pl.when(to != head)
+            def _():
+                part = pl.ds(pl.multiple_of(to * ROWS, ROWS), ROWS)
+                remote(merged.at[part], out_ref.at[:, my_columns], out_send, out_recv, seg, to).start()
+
+            return carry
+
+        lax.fori_loop(0, 4, send_out, 0)
+        return carry
+
+    lax.fori_loop(0, 4, merge, 0)
     pltpu.make_async_copy(merged.at[mine], out_ref.at[:, my_columns], out_recv).start()
 
     drain(full.at[2, others], in_send.at[2])
     for kv in range(2):
         drain(own1.at[kv], one_send.at[kv])
-        drain(gx.at[kv, pl.ds(0, NX - 1)], x_send.at[kv])
+        for n in range(3):
+            drain(gx.at[kv, 0], x_send.at[kv, n])
         for level in range(3, 6):
             drain(yk.at[kv, level - 3, pl.ds(0, COLUMN_KEYS - rows_of(level))], y_send.at[kv, level - 3])
     drain(qx.at[pl.ds(0, NX - 1)], q_send)
     drain(back_o.at[pl.ds(0, NX - 1)], back_send.at[0])
     drain(back_s.at[pl.ds(0, NX - 1)], back_send.at[1])
+    drain(off_tiles.at[pl.ds(0, HEADS - 1)], off_send)
+    drain(up_out.at[pl.ds(0, HEADS - 1)], up_send)
     drain(merged.at[others], out_send)
     drain(out_ref, out_recv)
 
@@ -341,6 +405,11 @@
         out_specs=pl.BlockSpec(memory_space=pl.ANY),
         scratch_shapes=[
             pltpu.SMEM((2, 6), jnp.int32),
+            pltpu.VMEM((HEADS, 4, WIDE), jnp.int32),
+            pltpu.VMEM((ROWS, D), BF),
+            pltpu.VMEM((UP_ROWS, HEADS * 16), BF),
+            pltpu.VMEM((HEADS, 16, WIDE), BF),
+            pltpu.VMEM((HEADS, 16, WIDE), BF),
             pltpu.VMEM((512, 256), BF),
             pltpu.VMEM((3, BLOCK, WIDE), BF),
             pltpu.VMEM((2, 512, WIDE), BF),
@@ -354,9 +423,9 @@
             pltpu.VMEM((NX, UP_ROWS, WIDE), BF),
             pltpu.VMEM((NX, STAT_ROWS, WIDE), F32),
             pltpu.VMEM((2, BLOCK, WIDE), BF),
-        ] + [pltpu.VMEM((BLOCK, WIDE), F32)] * 6 + [
+        ] + [pltpu.VMEM((BLOCK, WIDE), F32)] * 3 + [pltpu.VMEM((2, BLOCK, WIDE), F32)] * 3 + [pltpu.VMEM((UP_ROWS, WIDE), F32)] * 3 + [
             pltpu.VMEM((BLOCK, WIDE), BF),
-            dma, dma((3,)), dma((3,)), dma((2,)), dma((2,)), dma((2,)), dma((2,)), dma((2, 3)), dma((2, 3)),
+            dma, dma, dma, dma, dma, dma, dma((3,)), dma((3,)), dma((2,)), dma((2,)), dma((2, 3)), dma((2, 3)), dma((2, 3)), dma((2, 3)),
             dma, dma, dma((2,)), dma((2,)), dma, dma,
         ],
         compiler_params=pltpu.CompilerParams(

time: 60.9 us -> 55.2 us (0.906)
  Pallas kernels: 60.1 us -> 54.4 us
    pallas_call x1, Pallas kernels: 60.1 us -> 54.4 us  [per_device(): pl.pallas_call(kernel, out_shape=jax.ShapeDtypeStruct(queries.shape, BF),...]
where the time goes in v4:
time: 55.2 us; the launch traced here: 55.1 us
  Pallas kernels  54.4 us (99%)
  local copies, waits for them, and re-layouts  0.71 us (1%)
    pallas_call x1, Pallas kernels, per_device(): pl.pallas_call(kernel, out_shape=jax.ShapeDtypeStruct(queries.shape, BF),...  54.4 us

profile of v4, /device:TPU:1, one launch (start us, length us, event | category | flops | bytes accessed | tf_op | source)
XLA Modules:
  0.0 55.1 jit_solution(7712217411445360177)
XLA Ops:
  0.0 54.4 %shard_map.46 = bf16[64,2048]{1,0:T(8,128)(2,1)S(1)} custom-call(s32[2,6]{1,0:T(2,128)} %off_hbm.1, bf16[64,2048]{1,0:T(8,128)(2,1)} %q_ref.1, bf16[64,2048]{1,0:T(8,128)(2,1)} %k_ref.1, bf16[64,2048]{1,0:T(8,128)(2,1)} %v_ref.1), custom_call_target="tpu_custom_call" | custom-call | flops 1100000000 | bytes 1100000 | tf_op jit(solution)/shard_map/pallas_call | solution.py:401
  54.4 0.7 %copy.6 = bf16[64,2048]{1,0:T(8,128)(2,1)} copy(bf16[64,2048]{1,0:T(8,128)(2,1)S(1)} %shard_map.46) | data formatting | bytes 524288

commit v5 on v4

--- a/solution.py
+++ b/solution.py
@@ -54,7 +54,7 @@
     return lax.dot_general(a, b, (((1,), (0,)), ((), ())), preferred_element_type=F32)
 
 
-def attend(q, k, v_low, v_high):
+def weigh(q, k):
     rows = q.shape[0]
     low = low_lanes(rows)
     zero = jnp.zeros_like(q)
@@ -63,11 +63,21 @@
     scores = dot_t(both, k)
     top = jnp.max(scores, axis=1, keepdims=True)
     probs = jnp.exp(scores - top).astype(BF)
+    return probs, jnp.where(low, top[:rows], top[rows:])
+
+
+def add_up_values(probs, v_low, v_high):
+    rows = probs.shape[0] // 2
+    low = low_lanes(rows)
     first = dot(probs[:rows], v_low)
     second = dot(probs[rows:], v_high)
     total = jnp.where(low, first, second)
-    denom = pltpu.roll(jnp.where(low, second, first), WIDE // 2, 1)
-    return total, denom, jnp.where(low, top[:rows], top[rows:])
+    return total, pltpu.roll(jnp.where(low, second, first), WIDE // 2, 1)
+
+
+def attend(q, k, v_low, v_high):
+    probs, top = weigh(q, k)
+    return *add_up_values(probs, v_low, v_high), top
 
 
 def with_ones(v):
@@ -78,7 +88,7 @@
 
 def kernel(
     off_hbm, q_ref, k_ref, v_ref, out_ref,
-    off_ref, off_tiles, q_here, gather_up, up_out, up_in, pick, full, own1, got1, gx, yk, qsel, qx, part_o, part_s, back_o, back_s, v_one,
+    off_ref, off_tiles, q_here, gather_up, up_out, up_in, pick, full, own1, got1, gx, yk, qsel, qx, part_p, part_t, part_o, part_s, back_o, back_s, v_one,
     acc, den, top, acc_e, den_e, top_e, up_o, up_d, up_t, merged,
     off_sem, q_sem, off_recv, off_send, up_recv, up_send, in_recv, in_send, one_recv, one_send, x_recv, x_send, y_recv, y_send,
     q_recv, q_send, back_recv, back_send, out_recv, out_send,
@@ -122,7 +132,7 @@
         ref = (k_ref, v_ref, q_ref)[a]
 
         def send_in(i, carry):
-            to = lax.rem(head + i, HEADS)
+            to = lax.rem(head + HEADS // 2 + lax.div(i, 2) * (1 - 2 * lax.rem(i, 2)), HEADS)
             columns = pl.ds(pl.multiple_of(to * WIDE, WIDE), WIDE)
             remote(ref.at[:, columns], full.at[a, mine], in_send.at[a], in_recv.at[a], seg, to).start()
             return carry
@@ -258,18 +268,21 @@
     pass_on(1)
 
     drain(qx.at[pl.ds(0, NX - 1)], q_recv)
+    for level in range(3, 6):
+        rows, at = rows_of(level), UP_AT[level]
+        drain(yk.at[0, level - 3, pl.ds(0, COLUMN_KEYS - rows)], y_recv.at[0, level - 3])
+        for n in range(NX):
+            part_p[n, 2 * at:2 * (at + rows)], part_t[n, at:at + rows] = weigh(qx[n, at:at + rows], yk[0, level - 3])
     group_lane = lax.rem(lanes_of(STAT_ROWS), WIDE // 2) // 8
     stats = [jnp.zeros((STAT_ROWS, WIDE), F32) for _ in range(NX)]
     for level in range(3, 6):
-        rows = rows_of(level)
-        for kv in range(2):
-            drain(yk.at[kv, level - 3, pl.ds(0, COLUMN_KEYS - rows)], y_recv.at[kv, level - 3])
-        at = UP_AT[level]
+        rows, at = rows_of(level), UP_AT[level]
+        drain(yk.at[1, level - 3, pl.ds(0, COLUMN_KEYS - rows)], y_recv.at[1, level - 3])
         v_low, v_high = with_ones(yk[1, level - 3])
         for n in range(NX):
-            total, denom, peak = attend(qx[n, at:at + rows], yk[0, level - 3], v_low, v_high)
+            total, denom = add_up_values(part_p[n, 2 * at:2 * (at + rows)], v_low, v_high)
             part_o[n, at:at + rows] = (total / denom).astype(BF)
-            lse = peak + jnp.log(denom)
+            lse = part_t[n, at:at + rows] + jnp.log(denom)
             for m in range(rows // STAT_ROWS):
                 stats[n] = jnp.where(
                     group_lane == at // STAT_ROWS + m, lse[m * STAT_ROWS:(m + 1) * STAT_ROWS], stats[n]
@@ -335,7 +348,7 @@
         return (t & ((1 << level) - 1)) == jnp.where(low_lanes(rows), off_ref[0, level], off_ref[1, level])
 
     def merge(i, carry):
-        quarter = lax.rem(lax.div(head, 4) + i, 4)
+        quarter = lax.rem(lax.div(head, 4) + 2 + i, 4)
         held = {}
         for level in range(3, 6):
             count = 256 >> level
@@ -418,6 +431,8 @@
             pltpu.VMEM((2, 3, COLUMN_KEYS, WIDE), BF),
             pltpu.VMEM((768, WIDE), BF),
             pltpu.VMEM((NX, UP_ROWS, WIDE), BF),
+            pltpu.VMEM((NX, 2 * UP_ROWS, COLUMN_KEYS), BF),
+            pltpu.VMEM((NX, UP_ROWS, WIDE), F32),
             pltpu.VMEM((NX, UP_ROWS, WIDE), BF),
             pltpu.VMEM((NX, STAT_ROWS, WIDE), F32),
             pltpu.VMEM((NX, UP_ROWS, WIDE), BF),

time: 55.2 us -> 53.1 us (0.962)
  Pallas kernels: 54.4 us -> 52.2 us
    pallas_call x1, Pallas kernels: 54.4 us -> 52.2 us  [per_device(): pl.pallas_call(kernel, out_shape=jax.ShapeDtypeStruct(queries.shape, BF),...]
where the time goes in v5:
time: 53.1 us; the launch traced here: 53 us
  Pallas kernels  52.2 us (98%)
  local copies, waits for them, and re-layouts  0.71 us (1%)
    pallas_call x1, Pallas kernels, per_device(): pl.pallas_call(kernel, out_shape=jax.ShapeDtypeStruct(queries.shape, BF),...  52.2 us

profile of v5, /device:TPU:1, one launch (start us, length us, event | category | flops | bytes accessed | tf_op | source)
XLA Modules:
  0.0 53.0 jit_solution(3604101855449527631)
XLA Ops:
  0.0 52.2 %shard_map.46 = bf16[64,2048]{1,0:T(8,128)(2,1)S(1)} custom-call(s32[2,6]{1,0:T(2,128)} %off_hbm.1, bf16[64,2048]{1,0:T(8,128)(2,1)} %q_ref.1, bf16[64,2048]{1,0:T(8,128)(2,1)} %k_ref.1, bf16[64,2048]{1,0:T(8,128)(2,1)} %v_ref.1), custom_call_target="tpu_custom_call" | custom-call | flops 1100000000 | bytes 1100000 | tf_op jit(solution)/shard_map/pallas_call | solution.py:414
  52.3 0.7 %copy.6 = bf16[64,2048]{1,0:T(8,128)(2,1)} copy(bf16[64,2048]{1,0:T(8,128)(2,1)S(1)} %shard_map.46) | data formatting | bytes 524288

commit v6 on v5

--- a/solution.py
+++ b/solution.py
@@ -148,7 +148,7 @@
     off_tiles[head] = tile
 
     def send_offsets(i, carry):
-        to = lax.rem(head + i, HEADS)
+        to = lax.rem(head + HEADS // 2 + lax.div(i, 2) * (1 - 2 * lax.rem(i, 2)), HEADS)
         remote(off_tiles.at[head], off_tiles.at[head], off_send, off_recv, seg, to).start()
         return carry
 
@@ -241,7 +241,7 @@
     drain(full.at[0, others], in_send.at[0])
 
     def send_up(i, carry):
-        to = lax.rem(head + i, HEADS)
+        to = lax.rem(head + HEADS // 2 + lax.div(i, 2) * (1 - 2 * lax.rem(i, 2)), HEADS)
         remote(up_out.at[to], up_in.at[head], up_send, up_recv, seg, to).start()
         return carry
 
@@ -348,7 +348,8 @@
         return (t & ((1 << level) - 1)) == jnp.where(low_lanes(rows), off_ref[0, level], off_ref[1, level])
 
     def merge(i, carry):
-        quarter = lax.rem(lax.div(head, 4) + 2 + i, 4)
+        apart = 2 + lax.div(i + 1, 2) * (2 * lax.rem(i + 1, 2) - 1)
+        quarter = lax.rem(lax.div(head, 4) + apart, 4)
         held = {}
         for level in range(3, 6):
             count = 256 >> level

time: 53.1 us -> 53 us (level)
  no operation moved by 1% of the time
where the time goes in v6:
time: 53 us; the launch traced here: 52.9 us
  Pallas kernels  52.2 us (98%)
  local copies, waits for them, and re-layouts  0.71 us (1%)
    pallas_call x1, Pallas kernels, per_device(): pl.pallas_call(kernel, out_shape=jax.ShapeDtypeStruct(queries.shape, BF),...  52.2 us

profile of v6, /device:TPU:1, one launch (start us, length us, event | category | flops | bytes accessed | tf_op | source)
XLA Modules:
  0.0 52.9 jit_solution(5538196211297963509)
XLA Ops:
  0.0 52.2 %shard_map.46 = bf16[64,2048]{1,0:T(8,128)(2,1)S(1)} custom-call(s32[2,6]{1,0:T(2,128)} %off_hbm.1, bf16[64,2048]{1,0:T(8,128)(2,1)} %q_ref.1, bf16[64,2048]{1,0:T(8,128)(2,1)} %k_ref.1, bf16[64,2048]{1,0:T(8,128)(2,1)} %v_ref.1), custom_call_target="tpu_custom_call" | custom-call | flops 1100000000 | bytes 1100000 | tf_op jit(solution)/shard_map/pallas_call | solution.py:415
  52.2 0.7 %copy.6 = bf16[64,2048]{1,0:T(8,128)(2,1)} copy(bf16[64,2048]{1,0:T(8,128)(2,1)S(1)} %shard_map.46) | data formatting | bytes 524288
